TPU v7x, 128 devices: a whole 4x4x4 slice. The times are simulated.
128 devices in a mesh: seq: 32 (over y, z, x_lo), wt: 4 (over x_hi, core).
Axes of the slice: x: 4 (x_hi: 2, x_lo: 2; x = x_hi * 2 + x_lo), y: 4, z: 4, core: 2. Of those that a mesh axis runs over, the one named last changes fastest.
Arguments:
- tokens: float32 [4, 4096, 1024], P(None, 'seq'), may hold values from -6 to 6
- start_flags: int32 [4, 32], P(None, 'seq'), may hold values from 0 to 1, as said below
- norm_one: float32 [1024], replicated, may hold values from 0.5 to 1.5
- w_in: bfloat16 [3, 1024, 1024], P(None, None, 'wt'), may hold values from -0.1875 to 0.1875
- w_conv: float32 [3, 1024], P(None, 'wt'), may hold values from -3 to 3
- w_out: bfloat16 [1024, 1024], P(None, 'wt'), may hold values from -0.1875 to 0.1875
- norm_two: float32 [1024], replicated, may hold values from 0.5 to 1.5
- w_gate: bfloat16 [1024, 4608], P(None, 'wt'), may hold values from -0.1875 to 0.1875
- w_up: bfloat16 [1024, 4608], P(None, 'wt'), may hold values from -0.1875 to 0.1875
- w_down: bfloat16 [1024, 4608], P(None, 'wt'), may hold values from -0.1875 to 0.1875
- cotangent: float32 [4, 4096, 1024], P(None, 'seq'), may hold values from -6 to 6
Outputs:
- result: float32 [4, 4096, 1024], P(None, 'seq')
- grad_tokens: float32 [4, 4096, 1024], P(None, 'seq')
- grad_norm_one: float32 [1024], replicated
- grad_w_in: float32 [3, 1024, 1024], P(None, 'seq', 'wt')
- grad_w_conv: float32 [3, 1024], P(None, 'wt')
- grad_w_out: float32 [1024, 1024], P('seq', 'wt')
- grad_norm_two: float32 [1024], replicated
- grad_w_gate: float32 [1024, 4608], P('seq', 'wt')
- grad_w_up: float32 [1024, 4608], P('seq', 'wt')
- grad_w_down: float32 [1024, 4608], P('seq', 'wt')
Inputs may be any that keep to these rules, and one draw needn't show every extreme that they name: start_flags[r, 0] is 1 for every row; in one row, drawn from the seed, no other entry is 1, so that row holds one sequence of all 4096 positions.
All inputs are finite; a program needn't handle non-finite values.
Results may differ from a plain program's by a relative error of at most 0.0093.
Values sent between devices are 32-bit elements; how exact they have to be, the bound alone decides.
A program may use at most 128 MiB of HBM per device.

v0:
```python
import jax
import jax.numpy as jnp
from jax import lax
from jax.sharding import PartitionSpec as P

epsilon = 1e-05


def shifted(array, axis, by):
    peers = lax.axis_size(axis)
    pairs = [(i, i + by) for i in range(peers) if 0 <= i + by < peers]
    return lax.ppermute(array, axis, pairs)


def on_device(
    tokens, start_flags, norm_one, w_in, w_conv, w_out, norm_two, w_gate, w_up, w_down, cotangent
):
    starting = (start_flags == 1)[:, :, None]
    scale_one = lax.rsqrt(jnp.mean(tokens * tokens, axis=-1, keepdims=True) + epsilon)
    act_in = (tokens * scale_one * norm_one).astype(jnp.bfloat16)
    projected = jnp.einsum("rtd,jde->jrte", act_in, w_in, preferred_element_type=jnp.float32)
    gate_b, gate_c, value_x = (projected[0], projected[1], projected[2])
    product_bx = gate_b * value_x
    carried = shifted(product_bx[:, -2:], "seq", 1)
    carried = jnp.where(starting, 0.0, carried)
    extended = jnp.concatenate([carried, product_bx], axis=1)
    conv_out = w_conv[0] * extended[:, :-2] + w_conv[1] * extended[:, 1:-1] + w_conv[2] * product_bx
    act_mix = (gate_c * conv_out).astype(jnp.bfloat16)
    branch = lax.psum(
        jnp.einsum("rtc,dc->rtd", act_mix, w_out, preferred_element_type=jnp.float32), "wt"
    )
    middle = tokens + branch
    scale_two = lax.rsqrt(jnp.mean(middle * middle, axis=-1, keepdims=True) + epsilon)
    act_ffn = (middle * scale_two * norm_two).astype(jnp.bfloat16)
    gate_pre = jnp.einsum("rtd,df->rtf", act_ffn, w_gate, preferred_element_type=jnp.float32)
    up_value = jnp.einsum("rtd,df->rtf", act_ffn, w_up, preferred_element_type=jnp.float32)
    silu_gate = jax.nn.silu(gate_pre)
    hidden = (silu_gate * up_value).astype(jnp.bfloat16)
    ffn_out = lax.psum(
        jnp.einsum("rtf,df->rtd", hidden, w_down, preferred_element_type=jnp.float32), "wt"
    )
    result = middle + ffn_out
    grad_f = cotangent.astype(jnp.bfloat16)
    grad_w_down = jnp.einsum("rtd,rtf->df", grad_f, hidden, preferred_element_type=jnp.float32)
    grad_hidden = jnp.einsum("rtd,df->rtf", grad_f, w_down, preferred_element_type=jnp.float32)
    sigmoid_gate = jax.nn.sigmoid(gate_pre)
    grad_up = (grad_hidden * silu_gate).astype(jnp.bfloat16)
    grad_gate = (
        grad_hidden * up_value * sigmoid_gate * (1.0 + gate_pre * (1.0 - sigmoid_gate))
    ).astype(jnp.bfloat16)
    grad_w_gate = jnp.einsum("rtd,rtf->df", act_ffn, grad_gate, preferred_element_type=jnp.float32)
    grad_w_up = jnp.einsum("rtd,rtf->df", act_ffn, grad_up, preferred_element_type=jnp.float32)
    partial_ffn = jnp.einsum(
        "rtf,df->rtd", grad_gate, w_gate, preferred_element_type=jnp.float32
    ) + jnp.einsum("rtf,df->rtd", grad_up, w_up, preferred_element_type=jnp.float32)
    grad_act_ffn = lax.psum(partial_ffn, "wt")
    weighted_two = grad_act_ffn * norm_two
    grad_norm_two = jnp.sum(grad_act_ffn * middle * scale_two, axis=(0, 1))
    grad_middle = (
        cotangent
        + scale_two * weighted_two
        - middle * scale_two**3 * jnp.mean(weighted_two * middle, axis=-1, keepdims=True)
    )
    grad_branch = grad_middle.astype(jnp.bfloat16)
    grad_w_out = jnp.einsum("rtd,rtc->dc", grad_branch, act_mix, preferred_element_type=jnp.float32)
    grad_mix = jnp.einsum("rtd,dc->rtc", grad_branch, w_out, preferred_element_type=jnp.float32)
    grad_c = grad_mix * conv_out
    grad_conv = grad_mix * gate_c
    send_back = jnp.where(starting, 0.0, grad_conv[:, :2])
    arriving = shifted(send_back, "seq", -1)
    ext_grad = jnp.concatenate([grad_conv, arriving], axis=1)
    grad_bx = w_conv[2] * grad_conv + w_conv[1] * ext_grad[:, 1:-1] + w_conv[0] * ext_grad[:, 2:]
    grad_w_conv = jnp.stack(
        [
            jnp.sum(grad_conv * extended[:, :-2], axis=(0, 1)),
            jnp.sum(grad_conv * extended[:, 1:-1], axis=(0, 1)),
            jnp.sum(grad_conv * product_bx, axis=(0, 1)),
        ]
    )
    grad_projected = jnp.stack([grad_bx * value_x, grad_c, grad_bx * gate_b]).astype(jnp.bfloat16)
    grad_w_in = jnp.einsum(
        "rtd,jrte->jde", act_in, grad_projected, preferred_element_type=jnp.float32
    )
    partial_in = jnp.einsum(
        "jrte,jde->rtd", grad_projected, w_in, preferred_element_type=jnp.float32
    )
    grad_act_in = lax.psum(partial_in, "wt")
    weighted_one = grad_act_in * norm_one
    grad_norm_one = jnp.sum(grad_act_in * tokens * scale_one, axis=(0, 1))
    grad_tokens = (
        grad_middle
        + scale_one * weighted_one
        - tokens * scale_one**3 * jnp.mean(weighted_one * tokens, axis=-1, keepdims=True)
    )
    grad_w_in, grad_w_out, grad_w_gate, grad_w_up, grad_w_down = (
        lax.psum_scatter(grad_w_in, "seq", scatter_dimension=1, tiled=True),
        lax.psum_scatter(grad_w_out, "seq", scatter_dimension=0, tiled=True),
        lax.psum_scatter(grad_w_gate, "seq", scatter_dimension=0, tiled=True),
        lax.psum_scatter(grad_w_up, "seq", scatter_dimension=0, tiled=True),
        lax.psum_scatter(grad_w_down, "seq", scatter_dimension=0, tiled=True),
    )
    grad_w_conv, grad_norm_one, grad_norm_two = lax.psum(
        (grad_w_conv, grad_norm_one, grad_norm_two), "seq"
    )
    return (
        result,
        grad_tokens,
        grad_norm_one,
        grad_w_in,
        grad_w_conv,
        grad_w_out,
        grad_norm_two,
        grad_w_gate,
        grad_w_up,
        grad_w_down,
    )


def solution(mesh):
    return jax.shard_map(
        on_device,
        mesh=mesh,
        in_specs=(
            P(None, "seq", None),
            P(None, "seq"),
            P(),
            P(None, None, "wt"),
            P(None, "wt"),
            P(None, "wt"),
            P(),
            P(None, "wt"),
            P(None, "wt"),
            P(None, "wt"),
            P(None, "seq", None),
        ),
        out_specs=(
            P(None, "seq", None),
            P(None, "seq", None),
            P(),
            P(None, "seq", "wt"),
            P(None, "wt"),
            P("seq", "wt"),
            P(),
            P("seq", "wt"),
            P("seq", "wt"),
            P("seq", "wt"),
        ),
        check_vma=False,
    )
```

profile of v0, /device:TPU:0, one launch (start us, length us, event | category | flops | bytes accessed | tf_op | source)
XLA Modules:
  0.0 1307.6 jit_solution(2530528703543069066)
XLA Ops:
  7.3 2.0 multiply_reduce_fusion.5
  9.2 0.3 copy-done.2
  9.6 2.5 fusion.19
  12.1 0.1 fusion.39
  12.2 3.6 collective-permute-start
  15.9 1.3 collective-permute-done
  17.2 0.1 broadcast_select_fusion
  17.2 1.0 multiply_convert_fusion.8
  18.2 0.7 copy-done.13
  18.9 1.8 fusion.32
  20.8 5.2 fusion
  26.1 57.8 %all-reduce.8.cloned.1.call-done = f32[4,128,1024]{2,1,0:T(8,128)} async-done(((f32[4,128,1024]{2,1,0:T(8,128)}), f32[4,128,1024]{2,1,0:T(8,128)}) %all-reduce.8.cloned.1.call-update) | async-done | bytes 2097168 | tf_op jit(solution)/shard_map/psum | solution.py:29
  83.8 2.5 multiply_reduce_fusion.4
  86.4 1.3 copy-done.4
  87.7 0.2 multiply_convert_fusion.3
  87.9 0.9 copy-done.29
  88.8 1.5 fusion.6
  90.4 0.1 copy-done.32
  90.5 3.4 multiply_convert_fusion.1
  93.9 1.6 fusion.4
  95.4 2.9 fusion.16
  98.4 58.4 %all-reduce.10.cloned.1.call-done = f32[4,128,1024]{2,1,0:T(8,128)} async-done(((f32[4,128,1024]{2,1,0:T(8,128)}), f32[4,128,1024]{2,1,0:T(8,128)}) %all-reduce.10.cloned.1.call-update) | async-done | bytes 2097168 | tf_op jit(solution)/shard_map/psum | solution.py:56
  156.8 2.3 multiply_reduce_fusion
  159.1 0.5 copy-done.15
  159.7 0.5 multiply_subtract_fusion.1
  160.2 0.5 copy-done.17
  160.7 0.4 fusion.30
  161.2 1.7 copy-done.8
  162.9 0.1 copy-done.12
  163.0 0.2 copy-done.18
  163.1 0.2 multiply_reduce_fusion.8
  163.4 0.1 slice_select_fusion
  163.5 1.6 collective-permute-start.1
  165.1 4.1 collective-permute-done.1
  169.1 0.2 fusion.40
  169.4 0.1 fusion.42
  169.4 0.6 copy-done.24
  170.0 0.1 copy-done.22
  170.2 2.7 convolution_bitcast_fusion.3
  172.9 5.0 copy.35
  177.9 0.0 all-reduce.14.cloned.1.call-start
  178.0 5.0 fusion.2
  183.0 2.4 convolution_bitcast_fusion.4
  185.5 0.0 reduce-scatter.7.cloned.1.call-start
  185.5 0.9 copy-done.14
  186.4 3.1 convolution_bitcast_fusion.5
  189.5 5.5 convolution_bitcast_fusion
  195.1 6.1 copy.51
  201.2 5.0 convolution_bitcast_fusion.2
  206.2 0.0 reduce-scatter.11.cloned.1.call-start
  206.3 5.1 convolution_bitcast_fusion.1
  211.4 0.6 copy-done.31
  212.0 0.6 dynamic-slice
  213.3 304.0 %all-reduce.12.cloned.1.call-done = f32[3,1024,256]{2,0,1:T(4,128)} async-done(((f32[3,1024,256]{2,0,1:T(4,128)}), f32[3,1024,256]{2,0,1:T(4,128)}) %all-reduce.12.cloned.1.call-update) | async-done | bytes 3145744
  517.3 0.9 constant_dynamic-slice_fusion
  518.2 0.7 copy.40
  518.9 94.4 %all-reduce.14.cloned.1.call-done = (f32[4,128,1024]{2,1,0:T(8,128)}, f32[4,128,1024]{2,1,0:T(8,128)}) async-done(((f32[4,128,1024]{2,1,0:T(8,128)}, f32[4,128,1024]{2,1,0:T(8,128)}), (f32[4,128,1024]{2,1,0:T(8,128)}, f32[4,128,1024]{2,1,0:T(8,128)})) %all-reduce.14.cloned.1.call-update) | async-done | bytes 4194320 | tf_op jit(solution)/shard_map/psum | solution.py:39
  613.2 4.2 add.87
  617.5 0.6 multiply_reduce_fusion.1
  618.1 158.4 %all-reduce.1 = (f32[1024]{0:T(1024)}, f32[3,256]{1,0:T(4,128)}, f32[1024]{0:T(1024)}) all-reduce(f32[1024]{0:T(1024)S(1)} %get-tuple-element.32, f32[3,256]{1,0:T(4,128)S(1)} %pad_maximum_fusion.5, f32[1024]{0:T(1024)S(1)} %get-tuple-element.30), channel_id=1, replica_groups=mesh['seq'=32,'wt'=4] {'seq'}, use_global_device_ids=true, to_apply=%region_9.10 | all-reduce | flops 2816 | bytes 22528 | tf_op jit(solution)/shard_map/psum | solution.py:102
  776.5 4.9 multiply_subtract_fusion
  781.4 172.1 %reduce-scatter.13.cloned.1.call-done = f32[32,1152]{1,0:T(8,128)} async-done(((f32[1024,1152]{1,0:T(8,128)}), f32[32,1152]{1,0:T(8,128)}) %reduce-scatter.13.cloned.1.call-update) | async-done | bytes 147472
  953.5 173.0 %reduce-scatter.9.cloned.1.call-done = f32[32,1152]{1,0:T(8,128)} async-done(((f32[1024,1152]{1,0:T(8,128)}), f32[32,1152]{1,0:T(8,128)}) %reduce-scatter.9.cloned.1.call-update) | async-done | bytes 147472 | tf_op jit(solution)/shard_map/reduce_scatter | solution.py:98
  1126.5 174.3 %reduce-scatter.11.cloned.1.call-done = f32[32,1152]{1,0:T(8,128)} async-done(((f32[1024,1152]{1,0:T(8,128)}), f32[32,1152]{1,0:T(8,128)}) %reduce-scatter.11.cloned.1.call-update) | async-done | bytes 147472 | tf_op jit(solution)/shard_map/reduce_scatter | solution.py:99
  (74 shorter events, 0.5 us)
Async XLA Ops:
  7.2 83.2 %copy-start = (bf16[1024,1152]{1,0:T(8,128)(2,1)S(1)}, bf16[1024,1152]{1,0:T(8,128)(2,1)}, u32[]{:S(2)}) copy-start(bf16[1024,1152]{1,0:T(8,128)(2,1)} %param.18) | copy-start | bytes 7077892
  7.2 2.0 copy-start.26
  7.2 76.6 %all-reduce.8.cloned.1.call-start = ((), (), s32[]{:S(2)}) async-start(), calls=%async_computation.4 | async-start | bytes 4194304 | tf_op jit(solution)/shard_map/psum | solution.py:29
  7.2 2.3 copy-start.2
  9.6 6.2 copy-start.28
  9.6 6.3 copy-start.30
  12.1 5.2 copy-start.7
  12.1 6.9 copy-start.16
  12.2 6.1 copy-start.11
  12.2 5.0 collective-permute-start
  18.2 0.7 copy-start.13
  20.8 136.1 %all-reduce.10.cloned.1.call-start = ((), (), s32[]{:S(2)}) async-start(), calls=%async_computation.5 | async-start | bytes 4194304 | tf_op jit(solution)/shard_map/psum | solution.py:56
  26.1 61.6 %copy-start.27 = (f32[1024]{0:T(1024)S(1)}, f32[1024]{0:T(1024)}, u32[]{:S(2)}) copy-start(f32[1024]{0:T(1024)} %param.17) | copy-start | bytes 12292
  86.4 1.3 copy-start.4
  86.4 2.4 copy-start.29
  88.8 1.7 copy-start.32
  93.9 1.6 copy-start.20
  93.9 1.6 copy-start.21
  98.3 58.5 %copy-start.5 = (f32[4,128,1024]{2,1,0:T(8,128)S(1)}, f32[4,128,1024]{2,1,0:T(8,128)}, u32[]{:S(2)}) copy-start(f32[4,128,1024]{2,1,0:T(8,128)} %copy-done.4) | copy-start | bytes 6291460
  98.4 418.9 %all-reduce.12.cloned.1.call-start = ((), (), s32[]{:S(2)}) async-start(), calls=%async_computation.10 | async-start | bytes 8388608
  156.8 2.3 copy-start.10
  156.8 2.9 copy-start.15
  159.7 1.0 copy-start.17
  160.7 2.7 copy-start.6
  160.7 2.2 copy-start.8
  160.7 2.3 copy-start.12
  160.7 2.4 copy-start.18
  163.4 6.8 copy-start.3
  163.5 5.7 collective-permute-start.1
  169.3 0.7 copy-start.24
  169.4 0.7 copy-start.22
  177.9 435.3 %all-reduce.14.cloned.1.call-start = ((), (), s32[]{:S(2)}) async-start(), calls=%async_computation.11 | async-start | bytes 8388608 | tf_op jit(solution)/shard_map/psum | solution.py:39
  178.0 5.1 copy-start.19
  178.0 5.1 copy-start.23
  178.0 5.1 copy-start.25
  185.4 0.9 copy-start.14
  185.5 595.9 %reduce-scatter.7.cloned.1.call-start = ((), (), s32[]{:S(2)}) async-start(), calls=%async_computation.6 | async-start | bytes 1081344 | tf_op jit(solution)/shard_map/reduce_scatter | solution.py:97
  189.5 764.0 %reduce-scatter.13.cloned.1.call-start = ((), (), s32[]{:S(2)}) async-start(), calls=%async_computation.9 | async-start | bytes 4866048
  201.2 925.3 %reduce-scatter.9.cloned.1.call-start = ((), (), s32[]{:S(2)}) async-start(), calls=%async_computation.7 | async-start | bytes 4866048 | tf_op jit(solution)/shard_map/reduce_scatter | solution.py:98
  206.2 1094.5 %reduce-scatter.11.cloned.1.call-start = ((), (), s32[]{:S(2)}) async-start(), calls=%async_computation.8 | async-start | bytes 4866048 | tf_op jit(solution)/shard_map/reduce_scatter | solution.py:99
  211.4 0.7 copy-start.31
  613.2 4.3 copy-start.9
  776.5 524.3 %copy-start.1 = (bf16[1024,1152]{1,0:T(8,128)(2,1)S(1)}, bf16[1024,1152]{1,0:T(8,128)(2,1)}, u32[]{:S(2)}) copy-start(bf16[1024,1152]{1,0:T(8,128)(2,1)} %param.18) | copy-start | bytes 7077892
Sparse Core Ops, SparseCore 0:
  20.9 62.9 all-reduce.7
  98.5 58.2 all-reduce.9
  178.0 339.2 all-reduce.11
  520.3 92.9 all-reduce.13
  616.1 161.7 reduce-scatter.6
  780.7 172.7 reduce-scatter.12
  956.5 169.9 reduce-scatter.8
  1129.4 171.2 reduce-scatter.10
where the time goes:
time: 1310 us
  waiting for transfers between devices  1040 us (79%)
  blocking collectives  158 us (12%)
  matrix products  48.2 us (4%)
  local copies, waits for them, and re-layouts  21.9 us (2%)
  other arithmetic  19.1 us (1%)
  between operations  15.1 us (1%)
    unnamed x10, waiting for transfers between devices  476 us
    reduce_scatter x1, waiting for transfers between devices, on_device(): lax.psum_scatter(grad_w_up, 'seq', scatter_dimension=0, tiled=True)  174 us
    reduce_scatter x1, waiting for transfers between devices, on_device(): lax.psum_scatter(grad_w_gate, 'seq', scatter_dimension=0, tiled=True)  173 us
    psum x1, blocking collectives, on_device(): lax.psum((grad_w_conv, grad_norm_one, grad_norm_two), 'seq')  158 us
    psum x1, waiting for transfers between devices, on_device(): lax.psum(jnp.einsum('rtf,df->rtd', hidden, w_down, preferred_element_type...  94.4 us
    psum x1, waiting for transfers between devices, on_device(): grad_act_ffn = lax.psum(partial_ffn, 'wt')  58.4 us
    psum x1, waiting for transfers between devices, on_device(): lax.psum(jnp.einsum('rtc,dc->rtd', act_mix, w_out, preferred_element_type...  57.8 us
  transfers between devices with their start and end apart: 10, of which 9 were waited for; matrix products, arithmetic and copies ran while one was open for 4% of the time, Pallas kernels for 0%

commit v1 on v0

v1 whole, which is shorter than its diff:
```python
import functools

import jax
import jax.numpy as jnp
from jax import lax
from jax.experimental import pallas as pl
from jax.experimental.pallas import tpu as pltpu
from jax.sharding import PartitionSpec as P

EPS = 1e-05
MESH = pl.DeviceIdType.MESH
F32 = jnp.float32
BF16 = jnp.bfloat16
NN = ((1,), (0,))
NT = ((1,), (1,))
TN = ((0,), (0,))

ROWS, TB, D, CH, HID = 4, 128, 1024, 256, 1152
POS = ROWS * TB
HALF = TB // 2
WIDTHS = (HID, HID, HID, 4 * CH)
TILES = ((0, 256), (256, 256), (512, 256), (768, 256), (1024, 128))


def mm(a, b, dims):
    return lax.dot_general(a, b, (dims, ((), ())), preferred_element_type=F32)


def kernel(
    flags, tokens, cotangent, w_in, w_out, w_gate, w_up, w_down, norm_one, norm_two, w_conv,
    result, grad_tokens, o_in, o_out, o_gate, o_up, o_down, o_small,
    tok, cot, win, wout, wg, wu, wd,
    act_in, proj, bxe, gce, conv, amix, mid, aff, hid, gg, gu, gf, gh, gbr, gproj, sbuf, hf, hb,
    part, c_recv, x_recv, a_recv,
    grads, rel1, fin1, rel2, fin2, last, small, ar,
    in_sem, out_sem, h_s, h_r, c_s, c_r, x_s, x_r, a_s, a_r,
    s1_s, s1_r, s2_s, s2_r, s3_s, s3_r, ar_s, ar_r, credit,
):
    s = lax.axis_index("seq")
    w = lax.axis_index("wt")
    y, z, l = s // 8, (s // 2) % 4, s % 2
    h, c = w // 2, w % 2

    def dev(y=y, z=z, l=l, h=h, c=c):
        return ((y * 4 + z) * 2 + l, h * 2 + c)

    def up(v, by=1):
        return (v + by) % 4

    plus = (dev(y=up(y)), dev(z=up(z)))
    minus = (dev(y=up(y, 3)), dev(z=up(z, 3)))
    across = dev(l=1 - l)
    far = dev(h=1 - h)
    mate = dev(c=1 - c)
    following = ((s + 1) % 32, w)
    previous = ((s + 31) % 32, w)

    def remote(src, dst, send, recv, to):
        copy = pltpu.make_async_remote_copy(
            src_ref=src, dst_ref=dst, send_sem=send, recv_sem=recv, device_id=to, device_id_type=MESH
        )
        copy.start()
        return copy

    loads = {}

    def load(name, src, dst):
        loads[name] = pltpu.make_async_copy(src, dst, in_sem.at[len(loads)])
        loads[name].start()

    load("tok", tokens, tok)
    load("win", w_in, win)
    load("wout", w_out, wout)
    load("cot", cotangent, cot)
    load("wd", w_down, wd)
    load("wg", w_gate, wg)
    load("wu", w_up, wu)

    barrier = pltpu.get_barrier_semaphore()
    partners = (
        plus + minus + (dev(y=up(y, 2)), dev(z=up(z, 2)), across, far, mate, following, previous)
    )
    for partner in partners:
        pl.semaphore_signal(barrier, inc=1, device_id=partner, device_id_type=MESH)

    small[...] = jnp.zeros_like(small)

    def rows_of(g):
        return pl.ds(g * 2 * TB, 2 * TB)

    keep = [1.0 - (flags[r, 0] == 1).astype(F32) for r in range(ROWS)]

    halo = {}

    def mixer_in(g):
        t = tok[2 * g : 2 * g + 2].reshape(2 * TB, D)
        scale = lax.rsqrt(jnp.mean(t * t, axis=-1, keepdims=True) + EPS)
        act = (t * scale * norm_one[...]).astype(BF16)
        act_in[rows_of(g)] = act
        for j in range(3):
            proj[j, rows_of(g)] = mm(act, win[j], NN)
        bx = proj[0, rows_of(g)] * proj[2, rows_of(g)]
        for k in range(2):
            bxe[2 * g + k, 8:] = bx[k * TB : (k + 1) * TB]

    def send_halo(g):
        for r in (2 * g, 2 * g + 1):
            halo[r] = remote(bxe.at[r, pl.ds(TB, 8)], hf.at[r], h_s.at[0, r], h_r.at[0, r], following)

    csend, xsend, asend = {}, {}, {}
    own = pl.ds(pl.multiple_of(c * HALF, HALF), HALF)
    other = pl.ds(pl.multiple_of((1 - c) * HALF, HALF), HALF)
    bank_of = (0, 1, 0, 1)

    def sum_begin(q, r):
        b = bank_of[q]
        csend[q, r] = remote(part.at[b, r, other], c_recv.at[b, r], c_s.at[q, r], c_r.at[q, r], mate)

    def sum_cross(q, r):
        b = bank_of[q]
        csend[q, r].wait_recv()
        part[b, r, own] = part[b, r, own] + c_recv[b, r]
        xsend[q, r] = remote(part.at[b, r, own], x_recv.at[(0, 1, 0, 2)[q], r], x_s.at[q, r], x_r.at[q, r], far)

    def sum_share(q, r):
        b = bank_of[q]
        xsend[q, r].wait()
        part[b, r, own] = part[b, r, own] + x_recv[(0, 1, 0, 2)[q], r]
        asend[q, r] = remote(part.at[b, r, own], a_recv.at[b, r], a_s.at[q, r], a_r.at[q, r], mate)

    def sum_end(q, r):
        b = bank_of[q]
        csend[q, r].wait_send()
        asend[q, r].wait()
        part[b, r, other] = a_recv[b, r]

    def mixer_out(g):
        for r in (2 * g, 2 * g + 1):
            rows = pl.ds(r * TB, TB)
            halo[r].wait()
            bxe[r, 0:8] = hf[r] * keep[r]
            total = (
                w_conv[0:1] * bxe[r, 6 : 6 + TB]
                + w_conv[1:2] * bxe[r, 7 : 7 + TB]
                + w_conv[2:3] * bxe[r, 8 : 8 + TB]
            )
            conv[rows] = total
            amix[rows] = (proj[1, rows] * total).astype(BF16)
        partial = mm(amix[rows_of(g)], wout[...], NT)
        for k in range(2):
            part[0, 2 * g + k] = partial[k * TB : (k + 1) * TB]
            sum_begin(0, 2 * g + k)

    def grad_hidden(g):
        value = cot[2 * g : 2 * g + 2].reshape(2 * TB, D).astype(BF16)
        gf[rows_of(g)] = value
        for n, width in TILES:
            gh[rows_of(g), n : n + width] = mm(value, wd[:, n : n + width], NN)

    def ffn(g):
        for r in (2 * g, 2 * g + 1):
            rows = pl.ds(r * TB, TB)
            m = tok[r] + part[0, r]
            mid[r] = m
            scale = lax.rsqrt(jnp.mean(m * m, axis=-1, keepdims=True) + EPS)
            aff[rows] = (m * scale * norm_two[...]).astype(BF16)
        act = aff[rows_of(g)]
        for n, width in TILES:
            at = (rows_of(g), pl.ds(n, width))
            gate = mm(act, wg[:, n : n + width], NN)
            upv = mm(act, wu[:, n : n + width], NN)
            sig = jax.nn.sigmoid(gate)
            silu = gate * sig
            grad = gh[at]
            hid[at] = (silu * upv).astype(BF16)
            gu[at] = (grad * silu).astype(BF16)
            gg[at] = (grad * upv * sig * (1.0 + gate * (1.0 - sig))).astype(BF16)

    def ffn_back(g):
        partial = mm(gg[rows_of(g)], wg[...], NT) + mm(gu[rows_of(g)], wu[...], NT)
        for k in range(2):
            part[1, 2 * g + k] = partial[k * TB : (k + 1) * TB]
            sum_begin(1, 2 * g + k)

    def ffn_out(g):
        partial = mm(hid[rows_of(g)], wd[...], NT)
        for k in range(2):
            part[1, 2 * g + k] = partial[k * TB : (k + 1) * TB]
            sum_begin(3, 2 * g + k)

    def product(slot, left, right, n, width):
        @pl.loop(0, 4)
        def _(i):
            columns = pl.ds(pl.multiple_of(i * 256, 256), 256)
            value = mm(left[:, columns], right, TN)
            grads[slot, i, :, :, :, n : n + width] = value.reshape(4, 2, 32, width)

    place = (y, z)

    def chunk(job, p, j, half=None):
        slot, width = job % 2, pl.ds(0, WIDTHS[job])
        cut = pl.ds(0, 4) if half is None else pl.ds(2 * half, 2)
        if p == 0:
            return grads.at[slot, j, cut, 0, :, width]
        return grads.at[slot, cut, j, 1, :, width]

    first = {}

    def ring_begin(job):
        slot, width = job % 2, pl.ds(0, WIDTHS[job])
        for p in range(2):
            i = place[p]
            if job >= 2:
                pl.semaphore_wait(credit.at[slot, p, 0], 1)
                pl.semaphore_wait(credit.at[slot, p, 1], 1)
            sems = lambda k: (s1_s.at[job, p, k], s1_r.at[job, p, k])
            first[job, p] = [
                remote(chunk(job, p, up(i, 2), 0), rel1.at[slot, p, 0, :, :, width], *sems(0), plus[p]),
                remote(chunk(job, p, up(i, 2), 1), rel1.at[slot, p, 1, :, :, width], *sems(1), minus[p]),
                remote(chunk(job, p, up(i), 1), fin1.at[slot, p, 0, pl.ds(2, 2), :, width], *sems(2), plus[p]),
                remote(chunk(job, p, up(i, 3), 0), fin1.at[slot, p, 1, pl.ds(0, 2), :, width], *sems(3), minus[p]),
            ]

    def ring_relay(job):
        slot, n = job % 2, WIDTHS[job]
        width = pl.ds(0, n)
        for p in range(2):
            i = place[p]
            copies = first[job, p]
            for k, j, half, to in ((0, up(i), 0, plus[p]), (1, up(i, 3), 1, minus[p])):
                copies[k].wait_recv()
                target = chunk(job, p, j, half)
                for m in range(2):
                    target[m] = target[m] + rel1[slot, p, k, m, :, :n]
                copies.append(
                    remote(
                        target, fin1.at[slot, p, k, pl.ds(2 * half, 2), :, width],
                        s1_s.at[job, p, 4 + k], s1_r.at[job, p, 4 + k], to,
                    )
                )

    second = {}

    def piece(job, p, j, half=None):
        slot, width = job % 2, pl.ds(0, WIDTHS[job])
        cut = pl.ds(0, 32) if half is None else pl.ds(16 * half, 16)
        if p == 0:
            return grads.at[slot, y, j, 0, cut, width]
        return grads.at[slot, j, z, 1, cut, width]

    def ring_turn(job):
        slot, n = job % 2, WIDTHS[job]
        width = pl.ds(0, n)
        for p in range(2):
            for k in (2, 3, 4, 5):
                first[job, p][k].wait_recv()
            mine = chunk(job, p, place[p])

            @pl.loop(0, 4)
            def _(m):
                mine[m] = mine[m] + fin1[slot, p, 0, m, :, :n] + fin1[slot, p, 1, m, :, :n]

            if job < 2:
                pl.semaphore_signal(credit.at[slot, p, 0], inc=1, device_id=minus[p], device_id_type=MESH)
                pl.semaphore_signal(credit.at[slot, p, 1], inc=1, device_id=plus[p], device_id_type=MESH)
            i = place[1 - p]
            sems = lambda k: (s2_s.at[job, p, k], s2_r.at[job, p, k])
            a, b = plus[1 - p], minus[1 - p]
            second[job, p] = [
                remote(piece(job, p, up(i, 2), 0), rel2.at[job, p, 0, :, width], *sems(0), a),
                remote(piece(job, p, up(i, 2), 1), rel2.at[job, p, 1, :, width], *sems(1), b),
                remote(piece(job, p, up(i), 1), fin2.at[job, p, 0, pl.ds(16, 16), width], *sems(2), a),
                remote(piece(job, p, up(i, 3), 0), fin2.at[job, p, 1, pl.ds(0, 16), width], *sems(3), b),
            ]

    def ring_relay_two(job):
        n = WIDTHS[job]
        width = pl.ds(0, n)
        for p in range(2):
            i = place[1 - p]
            copies = second[job, p]
            for k, j, half, to in ((0, up(i), 0, plus[1 - p]), (1, up(i, 3), 1, minus[1 - p])):
                copies[k].wait_recv()
                target = piece(job, p, j, half)
                target[...] = target[...] + rel2[job, p, k, :, :n]
                copies.append(
                    remote(
                        target, fin2.at[job, p, k, pl.ds(16 * half, 16), width],
                        s2_s.at[job, p, 4 + k], s2_r.at[job, p, 4 + k], to,
                    )
                )

    third = {}

    def ring_cross(job):
        slot, n = job % 2, WIDTHS[job]
        width = pl.ds(0, n)
        for p in range(2):
            for k in (2, 3, 4, 5):
                second[job, p][k].wait_recv()
            mine = piece(job, p, place[1 - p])
            mine[...] = mine[...] + fin2[job, p, 0, :, :n] + fin2[job, p, 1, :, :n]
        third[job] = remote(
            grads.at[slot, y, z, 1 - l, :, width], last.at[job, :, width], s3_s.at[job], s3_r.at[job], across
        )

    def ring_end(job):
        slot, n = job % 2, WIDTHS[job]
        third[job].wait()
        total = grads[slot, y, z, l, :, :n] + last[job, :, :n]
        if job < 3:
            (o_down, o_gate, o_up)[job][...] = total
        else:
            for j in range(3):
                o_in[j] = total[:, j * CH : (j + 1) * CH]
            o_out[...] = total[:, 3 * CH :]

    def ring_sent(job):
        for p in range(2):
            for copy in first[job, p] + second[job, p]:
                copy.wait_send()

    back = {}

    def mixer_back(g):
        for r in (2 * g, 2 * g + 1):
            rows = pl.ds(r * TB, TB)
            m, grad = mid[r], part[1, r]
            scale = lax.rsqrt(jnp.mean(m * m, axis=-1, keepdims=True) + EPS)
            small[0:1] += jnp.sum(grad * m * scale, axis=0, keepdims=True)
            weighted = grad * norm_two[...]
            total = (
                cot[r]
                + scale * weighted
                - m * (scale * scale * scale) * jnp.mean(weighted * m, axis=-1, keepdims=True)
            )
            cot[r] = total
            gbr[rows] = total.astype(BF16)
        gmix = mm(gbr[rows_of(g)], wout[...], NN)
        for k in range(2):
            r = 2 * g + k
            rows = pl.ds(r * TB, TB)
            value = gmix[k * TB : (k + 1) * TB]
            gproj[1, rows] = (value * conv[rows]).astype(BF16)
            gce[r, 0:TB] = value * proj[1, rows]
            sbuf[r] = gce[r, 0:8] * keep[r]
            back[r] = remote(sbuf.at[r], hb.at[r], h_s.at[1, r], h_r.at[1, r], previous)

    def mixer_back_in(g):
        for r in (2 * g, 2 * g + 1):
            rows = pl.ds(r * TB, TB)
            back[r].wait()
            gce[r, TB:] = hb[r]
            value = gce[r, 0:TB]
            for k in range(3):
                small[2 + k : 3 + k, 0:CH] += jnp.sum(
                    value * bxe[r, 6 + k : 6 + k + TB], axis=0, keepdims=True
                )
            gbx = w_conv[2:3] * value + w_conv[1:2] * gce[r, 1 : 1 + TB] + w_conv[0:1] * gce[r, 2 : 2 + TB]
            gproj[0, rows] = (gbx * proj[2, rows]).astype(BF16)
            gproj[2, rows] = (gbx * proj[0, rows]).astype(BF16)
        partial = mm(gproj[0, rows_of(g)], win[0], NT)
        for j in (1, 2):
            partial += mm(gproj[j, rows_of(g)], win[j], NT)
        for k in range(2):
            part[0, 2 * g + k] = partial[k * TB : (k + 1) * TB]
            sum_begin(2, 2 * g + k)

    outs = []

    def tokens_out(r):
        t, grad = tok[r], part[0, r]
        scale = lax.rsqrt(jnp.mean(t * t, axis=-1, keepdims=True) + EPS)
        small[1:2] += jnp.sum(grad * t * scale, axis=0, keepdims=True)
        weighted = grad * norm_one[...]
        cot[r] = (
            cot[r]
            + scale * weighted
            - t * (scale * scale * scale) * jnp.mean(weighted * t, axis=-1, keepdims=True)
        )
        outs.append(pltpu.make_async_copy(cot.at[r], grad_tokens.at[r], out_sem.at[r]))
        outs[-1].start()

    def result_out(r):
        mid[r] = mid[r] + part[1, r]
        outs.append(pltpu.make_async_copy(mid.at[r], result.at[r], out_sem.at[4 + r]))
        outs[-1].start()

    reduced = {}

    def small_begin(stage):
        at, peers = (
            (y, [dev(y=up(y, k)) for k in (1, 2, 3)]),
            (z, [dev(z=up(z, k)) for k in (1, 2, 3)]),
            (l, [across]),
        )[stage]
        ar[stage, at] = small[...]
        reduced[stage] = [
            remote(small, ar.at[stage, at], ar_s.at[stage, k], ar_r.at[stage, at], to)
            for k, to in enumerate(peers)
        ]

    def small_end(stage):
        at, count = ((y, 4), (z, 4), (l, 2))[stage]
        for k, copy in enumerate(reduced[stage]):
            copy.wait_send()
            there = (at + k + 1) % count
            pltpu.make_async_remote_copy(
                src_ref=small, dst_ref=ar.at[stage, there], send_sem=ar_s.at[stage, k],
                recv_sem=ar_r.at[stage, there], device_id=mate, device_id_type=MESH,
            ).wait_recv()
        total = ar[stage, 0] + ar[stage, 1]
        for k in range(2, count):
            total += ar[stage, k]
        small[...] = total

    loads["tok"].wait()
    loads["win"].wait()
    mixer_in(0)
    mixer_in(1)
    pl.semaphore_wait(barrier, len(partners))
    send_halo(0)
    send_halo(1)
    loads["wout"].wait()
    mixer_out(0)
    mixer_out(1)
    for r in range(4):
        sum_cross(0, r)
    loads["cot"].wait()
    loads["wd"].wait()
    grad_hidden(0)
    grad_hidden(1)
    loads["wg"].wait()
    loads["wu"].wait()
    sum_share(0, 0)
    sum_share(0, 1)
    sum_end(0, 0)
    sum_end(0, 1)
    ffn(0)
    ffn_back(0)
    sum_share(0, 2)
    sum_share(0, 3)
    sum_cross(1, 0)
    sum_cross(1, 1)
    sum_end(0, 2)
    sum_end(0, 3)
    ffn(1)
    product(0, gf, hid[...], 0, HID)
    ring_begin(0)
    ffn_back(1)
    sum_cross(1, 2)
    sum_cross(1, 3)
    product(1, aff, gg[...], 0, HID)
    ring_begin(1)
    sum_share(1, 0)
    sum_share(1, 1)
    sum_end(1, 0)
    sum_end(1, 1)
    mixer_back(0)
    mixer_back_in(0)
    sum_cross(2, 0)
    sum_cross(2, 1)
    ring_relay(0)
    sum_share(1, 2)
    sum_share(1, 3)
    sum_end(1, 2)
    sum_end(1, 3)
    mixer_back(1)
    mixer_back_in(1)
    sum_cross(2, 2)
    sum_cross(2, 3)
    ring_turn(0)
    ffn_out(0)
    ffn_out(1)
    ring_relay_two(0)
    ring_relay(1)
    for r in range(4):
        sum_cross(3, r)
    ring_cross(0)
    ring_end(0)
    ring_sent(0)
    product(0, aff, gu[...], 0, HID)
    ring_begin(2)
    for r in range(4):
        sum_share(2, r)
    for r in range(4):
        sum_end(2, r)
        tokens_out(r)
    small_begin(0)
    ring_turn(1)
    small_end(0)
    small_begin(1)
    ring_relay_two(1)
    small_end(1)
    small_begin(2)
    ring_cross(1)
    ring_end(1)
    small_end(2)
    ring_sent(1)
    for j in range(3):
        product(1, act_in, gproj[j], j * CH, CH)
    product(1, gbr, amix[...], 3 * CH, CH)
    ring_begin(3)
    o_small[...] = small[...]
    ring_relay(2)
    for r in range(4):
        sum_share(3, r)
    for r in range(4):
        sum_end(3, r)
        result_out(r)
    ring_turn(2)
    ring_relay_two(2)
    ring_relay(3)
    ring_cross(2)
    ring_turn(3)
    ring_end(2)
    ring_relay_two(3)
    ring_sent(2)
    ring_cross(3)
    ring_end(3)
    ring_sent(3)
    for copy in outs:
        copy.wait()


def on_device(
    tokens, start_flags, norm_one, w_in, w_conv, w_out, norm_two, w_gate, w_up, w_down, cotangent
):
    any_spec = pl.BlockSpec(memory_space=pl.ANY)
    vmem = pl.BlockSpec(memory_space=pltpu.VMEM)
    dma = pltpu.SemaphoreType.DMA
    shape = jax.ShapeDtypeStruct
    outs = pl.pallas_call(
        kernel,
        out_shape=(
            shape((ROWS, TB, D), F32),
            shape((ROWS, TB, D), F32),
            shape((3, 32, CH), F32),
            shape((32, CH), F32),
            shape((32, HID), F32),
            shape((32, HID), F32),
            shape((32, HID), F32),
            shape((8, D), F32),
        ),
        in_specs=[pl.BlockSpec(memory_space=pltpu.SMEM)] + [any_spec] * 7 + [vmem] * 3,
        out_specs=(any_spec, any_spec) + (vmem,) * 6,
        scratch_shapes=[
            pltpu.VMEM((ROWS, TB, D), F32),
            pltpu.VMEM((ROWS, TB, D), F32),
            pltpu.VMEM((3, D, CH), BF16),
            pltpu.VMEM((D, CH), BF16),
            pltpu.VMEM((D, HID), BF16),
            pltpu.VMEM((D, HID), BF16),
            pltpu.VMEM((D, HID), BF16),
            pltpu.VMEM((POS, D), BF16),
            pltpu.VMEM((3, POS, CH), F32),
            pltpu.VMEM((ROWS, TB + 8, CH), F32),
            pltpu.VMEM((ROWS, TB + 8, CH), F32),
            pltpu.VMEM((POS, CH), F32),
            pltpu.VMEM((POS, CH), BF16),
            pltpu.VMEM((ROWS, TB, D), F32),
            pltpu.VMEM((POS, D), BF16),
            pltpu.VMEM((POS, HID), BF16),
            pltpu.VMEM((POS, HID), BF16),
            pltpu.VMEM((POS, HID), BF16),
            pltpu.VMEM((POS, D), BF16),
            pltpu.VMEM((POS, HID), F32),
            pltpu.VMEM((POS, D), BF16),
            pltpu.VMEM((3, POS, CH), BF16),
            pltpu.VMEM((ROWS, 8, CH), F32),
            pltpu.VMEM((ROWS, 8, CH), F32),
            pltpu.VMEM((ROWS, 8, CH), F32),
            pltpu.VMEM((2, ROWS, TB, D), F32),
            pltpu.VMEM((2, ROWS, HALF, D), F32),
            pltpu.VMEM((3, ROWS, HALF, D), F32),
            pltpu.VMEM((2, ROWS, HALF, D), F32),
            pltpu.VMEM((2, 4, 4, 2, 32, HID), F32),
            pltpu.VMEM((2, 2, 2, 2, 32, HID), F32),
            pltpu.VMEM((2, 2, 2, 4, 32, HID), F32),
            pltpu.VMEM((4, 2, 2, 16, HID), F32),
            pltpu.VMEM((4, 2, 2, 32, HID), F32),
            pltpu.VMEM((4, 32, HID), F32),
            pltpu.VMEM((8, D), F32),
            pltpu.VMEM((3, 4, 8, D), F32),
            dma((7,)),
            dma((8,)),
            dma((2, 4)),
            dma((2, 4)),
            dma((4, 4)),
            dma((4, 4)),
            dma((4, 4)),
            dma((4, 4)),
            dma((4, 4)),
            dma((4, 4)),
            dma((4, 2, 6)),
            dma((4, 2, 6)),
            dma((4, 2, 6)),
            dma((4, 2, 6)),
            dma((4,)),
            dma((4,)),
            dma((3, 3)),
            dma((3, 4)),
            pltpu.SemaphoreType.REGULAR((2, 2, 2)),
        ],
        compiler_params=pltpu.CompilerParams(
            collective_id=0, has_side_effects=True, vmem_limit_bytes=63 * 2**20
        ),
        name="block",
    )(
        start_flags, tokens, cotangent, w_in, w_out, w_gate, w_up, w_down,
        norm_one.reshape(1, D), norm_two.reshape(1, D), w_conv,
    )
    result, grad_tokens, g_in, g_out, g_gate, g_up, g_down, g_small = outs
    return (
        result, grad_tokens, g_small[1], g_in, g_small[2:5, :CH], g_out, g_small[0], g_gate, g_up, g_down,
    )


def solution(mesh):
    return jax.shard_map(
        on_device,
        mesh=mesh,
        in_specs=(
            P(None, "seq", None),
            P(None, "seq"),
            P(),
            P(None, None, "wt"),
            P(None, "wt"),
            P(None, "wt"),
            P(),
            P(None, "wt"),
            P(None, "wt"),
            P(None, "wt"),
            P(None, "seq", None),
        ),
        out_specs=(
            P(None, "seq", None),
            P(None, "seq", None),
            P(),
            P(None, "seq", "wt"),
            P(None, "wt"),
            P("seq", "wt"),
            P(),
            P("seq", "wt"),
            P("seq", "wt"),
            P("seq", "wt"),
        ),
        check_vma=False,
    )
```

time: 1310 us -> 219 us (0.17)
  waiting for transfers between devices: 1040 us -> 0 us
  Pallas kernels: 0 us -> 206 us
  blocking collectives: 158 us -> 0 us
  matrix products: 48.2 us -> 0 us
  other arithmetic: 19.1 us -> 0 us
  between operations: 15.1 us -> 0.68 us
    unnamed x10 -> x0, waiting for transfers between devices: 476 us -> none
    reduce_scatter x3 -> x0, waiting for transfers between devices: 347 us -> none  [the longest x1 174 us: on_device(): lax.psum_scatter(grad_w_up, 'seq', scatter_dimension=0, tiled=True)]
    psum x3 -> x0, waiting for transfers between devices: 211 us -> none  [the longest x1 94.4 us: on_device(): lax.psum(jnp.einsum('rtf,df->rtd', hidden, w_down, preferred_element_type...]
    pallas_call x0 -> x1, Pallas kernels: none -> 206 us  [on_device(): pl.pallas_call(kernel, out_shape=(shape((ROWS, TB, D), F32), shape((ROWS,...]
    psum x1 -> x0, blocking collectives: 158 us -> none  [on_device(): lax.psum((grad_w_conv, grad_norm_one, grad_norm_two), 'seq')]
    dot_general x15 -> x0, matrix products: 48.2 us -> none  [the longest x1 5.55 us: on_device(): jnp.einsum('rtd,rtf->df', grad_f, hidden, preferred_element_type=jnp.floa...]
  transfers between devices with their start and end apart: 10 -> 0, of which waited for: 9 -> 0; matrix products, arithmetic and copies ran while one was open for 4% -> 0% of each run, Pallas kernels for 0% -> 0%
where the time goes in v1:
time: 219 us; the launch traced here: 218 us
  Pallas kernels  206 us (94%)
  local copies, waits for them, and re-layouts  11.9 us (5%)
    pallas_call x1, Pallas kernels, on_device(): pl.pallas_call(kernel, out_shape=(shape((ROWS, TB, D), F32), shape((ROWS,...  206 us
    unnamed x20, local copies, waits for them, and re-layouts  9.2 us

profile of v1, /device:TPU:0, one launch (start us, length us, event | category | flops | bytes accessed | tf_op | source)
XLA Modules:
  0.0 218.3 jit_solution(11280791496793633470)
XLA Ops:
  0.6 1.3 copy.21.flags
  2.0 205.7 %block.1 = (f32[4,128,1024]{2,1,0:T(8,128)}, f32[4,128,1024]{2,1,0:T(8,128)}, f32[3,32,256]{2,1,0:T(8,128)}, f32[32,256]{1,0:T(8,128)}, f32[32,1152]{1,0:T(8,128...) custom-call(s32[4,1]{1,0:T(4,128)} %copy.21.flags, f32[4,128,1024]{2,1,0:T(8,128)} %tokens.1, ...), custom_call_target="tpu_custom_call" | custom-call | tf_op jit(solution)/shard_map/block/pallas_call | solution.py:533
  207.6 1.4 fusion
  209.1 1.3 slice.10
  210.3 0.0 copy-start
  210.3 3.3 %copy.29 = f32[4,128,1024]{2,1,0:T(8,128)} copy(f32[4,128,1024]{2,1,0:T(8,128)} %get-tuple-element.38) | data formatting | bytes 4194304
  213.7 0.0 copy-done
  213.7 0.0 copy-start.4
  213.7 0.0 copy-start.5
  213.7 0.0 copy-start.3
  213.7 0.0 copy-start.2
  213.7 0.0 copy-start.1
  213.7 1.3 copy.30
  215.0 0.0 copy-done.4
  215.0 0.6 copy.31
  215.7 0.0 copy-done.5
  215.7 0.6 copy.32
  216.3 0.0 copy-done.3
  216.3 0.7 copy.33
  216.9 0.0 copy-done.2
  216.9 0.7 copy.34
  217.6 0.0 copy-done.1
  217.6 0.7 copy.35
Async XLA Ops:
  210.3 3.3 %copy-start = (f32[4,128,1024]{2,1,0:T(8,128)S(1)}, f32[4,128,1024]{2,1,0:T(8,128)}, u32[]{:S(2)}) copy-start(f32[4,128,1024]{2,1,0:T(8,128)} %get-tuple-element.39) | copy-start | bytes 6291460
  213.7 1.4 copy-start.4
  213.7 2.0 copy-start.5
  213.7 2.6 %copy-start.3 = (f32[32,1152]{1,0:T(8,128)S(1)}, f32[32,1152]{1,0:T(8,128)}, u32[]{:S(2)}) copy-start(f32[32,1152]{1,0:T(8,128)} %get-tuple-element.45) | copy-start | bytes 442372
  213.7 3.3 %copy-start.2 = (f32[32,1152]{1,0:T(8,128)S(1)}, f32[32,1152]{1,0:T(8,128)}, u32[]{:S(2)}) copy-start(f32[32,1152]{1,0:T(8,128)} %get-tuple-element.46) | copy-start | bytes 442372
  213.7 3.9 %copy-start.1 = (f32[32,1152]{1,0:T(8,128)S(1)}, f32[32,1152]{1,0:T(8,128)}, u32[]{:S(2)}) copy-start(f32[32,1152]{1,0:T(8,128)} %get-tuple-element.47) | copy-start | bytes 442372

commit v2 on v1

--- a/solution.py
+++ b/solution.py
@@ -18,7 +18,13 @@
 ROWS, TB, D, CH, HID = 4, 128, 1024, 256, 1152
 POS = ROWS * TB
 HALF = TB // 2
-WIDTHS = (HID, HID, HID, 4 * CH)
+JOBS = (
+    (0, 0, HID, 32),
+    (1, 0, HID, 32),
+    (0, 0, HID, 32),
+    (1, 0, 3 * CH, 32),
+    (1, 3 * CH, CH, 16),
+)
 TILES = ((0, 256), (256, 256), (512, 256), (768, 256), (1024, 128))
 
 
@@ -30,11 +36,11 @@
     flags, tokens, cotangent, w_in, w_out, w_gate, w_up, w_down, norm_one, norm_two, w_conv,
     result, grad_tokens, o_in, o_out, o_gate, o_up, o_down, o_small,
     tok, cot, win, wout, wg, wu, wd,
-    act_in, proj, bxe, gce, conv, amix, mid, aff, hid, gg, gu, gf, gh, gbr, gproj, sbuf, hf, hb,
+    proj, bxe, gce, mid, aff, hid, gg, gu, gf, gh, sbuf, hf, hb,
     part, c_recv, x_recv, a_recv,
-    grads, rel1, fin1, rel2, fin2, last, small, ar,
-    in_sem, out_sem, h_s, h_r, c_s, c_r, x_s, x_r, a_s, a_r,
-    s1_s, s1_r, s2_s, s2_r, s3_s, s3_r, ar_s, ar_r, credit,
+    grads, rel1, fin1, rel2, fin2, last, grads_out, paired, small, ar,
+    in_sem, out_sem, m_s, m_r, v_s, v_r, h_s, h_r, c_s, c_r, x_s, x_r, a_s, a_r,
+    s1_s, s1_r, s2_s, s2_r, s3_s, s3_r, p_s, p_r, ar_s, ar_r, credit,
 ):
     s = lax.axis_index("seq")
     w = lax.axis_index("wt")
@@ -68,9 +74,9 @@
         loads[name] = pltpu.make_async_copy(src, dst, in_sem.at[len(loads)])
         loads[name].start()
 
+    load("wout", w_out, wout)
     load("tok", tokens, tok)
     load("win", w_in, win)
-    load("wout", w_out, wout)
     load("cot", cotangent, cot)
     load("wd", w_down, wd)
     load("wg", w_gate, wg)
@@ -88,15 +94,17 @@
     def rows_of(g):
         return pl.ds(g * 2 * TB, 2 * TB)
 
-    keep = [1.0 - (flags[r, 0] == 1).astype(F32) for r in range(ROWS)]
+    keep = [1.0 - (flags[0, r] == 1).astype(F32) for r in range(ROWS)]
 
     halo = {}
 
-    def mixer_in(g):
+    def normed(g):
         t = tok[2 * g : 2 * g + 2].reshape(2 * TB, D)
         scale = lax.rsqrt(jnp.mean(t * t, axis=-1, keepdims=True) + EPS)
-        act = (t * scale * norm_one[...]).astype(BF16)
-        act_in[rows_of(g)] = act
+        return (t * scale * norm_one[...]).astype(BF16)
+
+    def mixer_in(g):
+        act = normed(g)
         for j in range(3):
             proj[j, rows_of(g)] = mm(act, win[j], NN)
         bx = proj[0, rows_of(g)] * proj[2, rows_of(g)]
@@ -107,10 +115,129 @@
         for r in (2 * g, 2 * g + 1):
             halo[r] = remote(bxe.at[r, pl.ds(TB, 8)], hf.at[r], h_s.at[0, r], h_r.at[0, r], following)
 
+    mine = pl.ds(pl.multiple_of(w * CH, CH), CH)
+    theirs = pl.ds(pl.multiple_of(((1 - h) * 2 + c) * CH, CH), CH)
+    weight = {}
+
+    def weight_begin():
+        @pl.loop(0, 4)
+        def _(i):
+            rows = pl.ds(pl.multiple_of(i * 256, 256), 256)
+            grads[1, i, :, :, :, mine] = wout[rows].astype(F32).reshape(4, 2, 32, CH)
+
+    def weight_far():
+        block = grads.at[1, y, z, :, :, mine]
+        weight["far"] = remote(block, block, v_s.at[0], v_r.at[0], far)
+        block = grads.at[1, :, :, :, :, mine]
+        weight["mate"] = remote(block, block, v_s.at[1], v_r.at[1], mate)
+
+    def weight_first():
+        weight["far"].wait_recv()
+        for p in range(2):
+            for k in (1, 2, 3):
+                to = dev(y=up(y, k)) if p == 0 else dev(z=up(z, k))
+                block = grads.at[1, y, z, p, :, theirs]
+                weight["first", p, k] = remote(
+                    block, block, v_s.at[1 + p * 3 + k], v_r.at[1 + p * 3 + k], to
+                )
+
+    def weight_row(p, j):
+        return grads.at[1, :, j, 0, :, theirs] if p == 0 else grads.at[1, j, :, 1, :, theirs]
+
+    def weight_pass(p, k):
+        block = weight_row(p, up((z, y)[p], 4 - k))
+        weight["pass", p, k] = remote(
+            block, block, v_s.at[14 + p * 4 + k], v_r.at[14 + p * 4 + k], mate
+        )
+
+    def weight_second():
+        for p in range(2):
+            for k in (1, 2, 3):
+                weight["first", p, k].wait_recv()
+        for p in range(2):
+            for k in (1, 2, 3):
+                to = dev(z=up(z, k)) if p == 0 else dev(y=up(y, k))
+                block = weight_row(p, (z, y)[p])
+                weight["second", p, k] = remote(
+                    block, block, v_s.at[7 + p * 3 + k], v_r.at[7 + p * 3 + k], to
+                )
+        for p in range(2):
+            weight_pass(p, 0)
+
+    def weight_third():
+        for k in (1, 3, 2):
+            for p in range(2):
+                weight["second", p, k].wait_recv()
+                weight_pass(p, k)
+
+    def weight_end():
+        weight["mate"].wait()
+        weight["far"].wait_send()
+        for p in range(2):
+            for k in (1, 2, 3):
+                weight["first", p, k].wait_send()
+                weight["second", p, k].wait_send()
+            for k in range(4):
+                weight["pass", p, k].wait()
+
+    mix = {}
+
+    def mix_block(k, columns):
+        if k < 4:
+            return part.at[0, k, pl.ds(8, TB - 8), columns]
+        return part.at[0, :, pl.ds(0, 8), columns]
+
+    def mix_send(k):
+        block = mix_block(k, mine)
+        mix["far", k] = remote(block, block, m_s.at[0, k], m_r.at[0, k], far)
+        mix["mate", k] = remote(block, block, m_s.at[1, k], m_r.at[1, k], mate)
+
+    def mix_pass(k):
+        mix["far", k].wait_recv()
+        block = mix_block(k, theirs)
+        mix["pass", k] = remote(block, block, m_s.at[2, k], m_r.at[2, k], mate)
+
+    def mix_end(k):
+        mix["far", k].wait_send()
+        mix["mate", k].wait()
+        mix["pass", k].wait()
+
+    def conv(r, at, count):
+        return (
+            w_conv[0:1] * bxe[r, at + 6 : at + 6 + count]
+            + w_conv[1:2] * bxe[r, at + 7 : at + 7 + count]
+            + w_conv[2:3] * bxe[r, at + 8 : at + 8 + count]
+        )
+
+    def taps(r, at, count):
+        total = conv(r, at, count)
+        rows = pl.ds(r * TB + at, count)
+        part[0, r, at : at + count, mine] = (proj[1, rows] * total).astype(BF16).astype(F32)
+
+    def mixer_out(g):
+        for r in (2 * g, 2 * g + 1):
+            taps(r, 8, TB - 8)
+            mix_send(r)
+
+    def mixer_edge():
+        for r in range(4):
+            halo[r].wait()
+            bxe[r, 0:8] = hf[r] * keep[r]
+            taps(r, 0, 8)
+        mix_send(4)
+
+    def branch(g):
+        left = part[0, 2 * g : 2 * g + 2].reshape(2 * TB, D).astype(BF16)
+        for i in range(4):
+            right = grads[1, i, :, :, :, 0:D].reshape(256, D).astype(BF16)
+            value = mm(left, right, NT).reshape(2, TB, 256)
+            columns = pl.ds(i * 256, 256)
+            mid[2 * g : 2 * g + 2, :, columns] = tok[2 * g : 2 * g + 2, :, columns] + value
+
     csend, xsend, asend = {}, {}, {}
     own = pl.ds(pl.multiple_of(c * HALF, HALF), HALF)
     other = pl.ds(pl.multiple_of((1 - c) * HALF, HALF), HALF)
-    bank_of = (0, 1, 0, 1)
+    bank_of = (None, 1, 0, 1)
 
     def sum_begin(q, r):
         b = bank_of[q]
@@ -120,12 +247,12 @@
         b = bank_of[q]
         csend[q, r].wait_recv()
         part[b, r, own] = part[b, r, own] + c_recv[b, r]
-        xsend[q, r] = remote(part.at[b, r, own], x_recv.at[(0, 1, 0, 2)[q], r], x_s.at[q, r], x_r.at[q, r], far)
+        xsend[q, r] = remote(part.at[b, r, own], x_recv.at[q - 1, r], x_s.at[q, r], x_r.at[q, r], far)
 
     def sum_share(q, r):
         b = bank_of[q]
         xsend[q, r].wait()
-        part[b, r, own] = part[b, r, own] + x_recv[(0, 1, 0, 2)[q], r]
+        part[b, r, own] = part[b, r, own] + x_recv[q - 1, r]
         asend[q, r] = remote(part.at[b, r, own], a_recv.at[b, r], a_s.at[q, r], a_r.at[q, r], mate)
 
     def sum_end(q, r):
@@ -134,23 +261,6 @@
         asend[q, r].wait()
         part[b, r, other] = a_recv[b, r]
 
-    def mixer_out(g):
-        for r in (2 * g, 2 * g + 1):
-            rows = pl.ds(r * TB, TB)
-            halo[r].wait()
-            bxe[r, 0:8] = hf[r] * keep[r]
-            total = (
-                w_conv[0:1] * bxe[r, 6 : 6 + TB]
-                + w_conv[1:2] * bxe[r, 7 : 7 + TB]
-                + w_conv[2:3] * bxe[r, 8 : 8 + TB]
-            )
-            conv[rows] = total
-            amix[rows] = (proj[1, rows] * total).astype(BF16)
-        partial = mm(amix[rows_of(g)], wout[...], NT)
-        for k in range(2):
-            part[0, 2 * g + k] = partial[k * TB : (k + 1) * TB]
-            sum_begin(0, 2 * g + k)
-
     def grad_hidden(g):
         value = cot[2 * g : 2 * g + 2].reshape(2 * TB, D).astype(BF16)
         gf[rows_of(g)] = value
@@ -160,8 +270,7 @@
     def ffn(g):
         for r in (2 * g, 2 * g + 1):
             rows = pl.ds(r * TB, TB)
-            m = tok[r] + part[0, r]
-            mid[r] = m
+            m = mid[r]
             scale = lax.rsqrt(jnp.mean(m * m, axis=-1, keepdims=True) + EPS)
             aff[rows] = (m * scale * norm_two[...]).astype(BF16)
         act = aff[rows_of(g)]
@@ -193,37 +302,60 @@
         def _(i):
             columns = pl.ds(pl.multiple_of(i * 256, 256), 256)
             value = mm(left[:, columns], right, TN)
-            grads[slot, i, :, :, :, n : n + width] = value.reshape(4, 2, 32, width)
+            value = value.reshape(4, 2, 32, width)
+            if slot is None:
+                grads_out[i] = value
+            else:
+                grads[slot, i, :, :, :, n : n + width] = value
 
     place = (y, z)
 
+    def block_of(job):
+        slot, at, n, deep = JOBS[job]
+        return slot, pl.ds(at, n), pl.ds(0, deep), deep
+
     def chunk(job, p, j, half=None):
-        slot, width = job % 2, pl.ds(0, WIDTHS[job])
+        slot, columns, rows, deep = block_of(job)
         cut = pl.ds(0, 4) if half is None else pl.ds(2 * half, 2)
+        if deep != 32:
+            rows = pl.ds(deep * p, deep)
+            return grads_out.at[j, cut, l, rows] if p == 0 else grads_out.at[cut, j, l, rows]
         if p == 0:
-            return grads.at[slot, j, cut, 0, :, width]
-        return grads.at[slot, cut, j, 1, :, width]
+            return grads.at[slot, j, cut, 0, rows, columns]
+        return grads.at[slot, cut, j, 1, rows, columns]
+
+    pair = []
+
+    def pair_begin():
+        pair.append(remote(grads_out.at[:, :, 1 - l], paired, p_s.at[0], p_r.at[0], across))
+
+    def pair_end():
+        pair[0].wait()
+
+        @pl.loop(0, 4)
+        def _(i):
+            grads_out[i, :, l] = grads_out[i, :, l] + paired[i]
 
     first = {}
 
     def ring_begin(job):
-        slot, width = job % 2, pl.ds(0, WIDTHS[job])
+        slot, columns, rows, _ = block_of(job)
         for p in range(2):
             i = place[p]
-            if job >= 2:
+            if job in (2, 3):
                 pl.semaphore_wait(credit.at[slot, p, 0], 1)
                 pl.semaphore_wait(credit.at[slot, p, 1], 1)
             sems = lambda k: (s1_s.at[job, p, k], s1_r.at[job, p, k])
+            a, b = plus[p], minus[p]
             first[job, p] = [
-                remote(chunk(job, p, up(i, 2), 0), rel1.at[slot, p, 0, :, :, width], *sems(0), plus[p]),
-                remote(chunk(job, p, up(i, 2), 1), rel1.at[slot, p, 1, :, :, width], *sems(1), minus[p]),
-                remote(chunk(job, p, up(i), 1), fin1.at[slot, p, 0, pl.ds(2, 2), :, width], *sems(2), plus[p]),
-                remote(chunk(job, p, up(i, 3), 0), fin1.at[slot, p, 1, pl.ds(0, 2), :, width], *sems(3), minus[p]),
+                remote(chunk(job, p, up(i, 2), 0), rel1.at[slot, p, 0, :, rows, columns], *sems(0), a),
+                remote(chunk(job, p, up(i, 2), 1), rel1.at[slot, p, 1, :, rows, columns], *sems(1), b),
+                remote(chunk(job, p, up(i), 1), fin1.at[slot, p, 0, pl.ds(2, 2), rows, columns], *sems(2), a),
+                remote(chunk(job, p, up(i, 3), 0), fin1.at[slot, p, 1, pl.ds(0, 2), rows, columns], *sems(3), b),
             ]
 
     def ring_relay(job):
-        slot, n = job % 2, WIDTHS[job]
-        width = pl.ds(0, n)
+        slot, columns, rows, _ = block_of(job)
         for p in range(2):
             i = place[p]
             copies = first[job, p]
@@ -231,10 +363,10 @@
                 copies[k].wait_recv()
                 target = chunk(job, p, j, half)
                 for m in range(2):
-                    target[m] = target[m] + rel1[slot, p, k, m, :, :n]
+                    target[m] = target[m] + rel1[slot, p, k, m, rows, columns]
                 copies.append(
                     remote(
-                        target, fin1.at[slot, p, k, pl.ds(2 * half, 2), :, width],
+                        target, fin1.at[slot, p, k, pl.ds(2 * half, 2), rows, columns],
                         s1_s.at[job, p, 4 + k], s1_r.at[job, p, 4 + k], to,
                     )
                 )
@@ -242,15 +374,15 @@
     second = {}
 
     def piece(job, p, j, half=None):
-        slot, width = job % 2, pl.ds(0, WIDTHS[job])
-        cut = pl.ds(0, 32) if half is None else pl.ds(16 * half, 16)
-        if p == 0:
-            return grads.at[slot, y, j, 0, cut, width]
-        return grads.at[slot, j, z, 1, cut, width]
+        slot, columns, _, deep = block_of(job)
+        row = (slot * 2 + p) * 128 + j * 32
+        if half is None:
+            return gh.at[pl.ds(pl.multiple_of(row, 32), deep), columns]
+        return gh.at[pl.ds(pl.multiple_of(row + deep // 2 * half, 8), deep // 2), columns]
 
     def ring_turn(job):
-        slot, n = job % 2, WIDTHS[job]
-        width = pl.ds(0, n)
+        slot, columns, rows, deep = block_of(job)
+        at, cut = min(job, 3), (pl.ds(0, deep // 2), pl.ds(deep // 2, deep // 2))
         for p in range(2):
             for k in (2, 3, 4, 5):
                 first[job, p][k].wait_recv()
@@ -258,7 +390,10 @@
 
             @pl.loop(0, 4)
             def _(m):
-                mine[m] = mine[m] + fin1[slot, p, 0, m, :, :n] + fin1[slot, p, 1, m, :, :n]
+                to = pl.ds(pl.multiple_of((slot * 2 + p) * 128 + m * 32, 32), deep)
+                gh[to, columns] = (
+                    mine[m] + fin1[slot, p, 0, m, rows, columns] + fin1[slot, p, 1, m, rows, columns]
+                )
 
             if job < 2:
                 pl.semaphore_signal(credit.at[slot, p, 0], inc=1, device_id=minus[p], device_id_type=MESH)
@@ -267,25 +402,25 @@
             sems = lambda k: (s2_s.at[job, p, k], s2_r.at[job, p, k])
             a, b = plus[1 - p], minus[1 - p]
             second[job, p] = [
-                remote(piece(job, p, up(i, 2), 0), rel2.at[job, p, 0, :, width], *sems(0), a),
-                remote(piece(job, p, up(i, 2), 1), rel2.at[job, p, 1, :, width], *sems(1), b),
-                remote(piece(job, p, up(i), 1), fin2.at[job, p, 0, pl.ds(16, 16), width], *sems(2), a),
-                remote(piece(job, p, up(i, 3), 0), fin2.at[job, p, 1, pl.ds(0, 16), width], *sems(3), b),
+                remote(piece(job, p, up(i, 2), 0), rel2.at[at, p, 0, cut[0], columns], *sems(0), a),
+                remote(piece(job, p, up(i, 2), 1), rel2.at[at, p, 1, cut[0], columns], *sems(1), b),
+                remote(piece(job, p, up(i), 1), fin2.at[at, p, 0, cut[1], columns], *sems(2), a),
+                remote(piece(job, p, up(i, 3), 0), fin2.at[at, p, 1, cut[0], columns], *sems(3), b),
             ]
 
     def ring_relay_two(job):
-        n = WIDTHS[job]
-        width = pl.ds(0, n)
+        _, columns, _, deep = block_of(job)
+        at, cut = min(job, 3), (pl.ds(0, deep // 2), pl.ds(deep // 2, deep // 2))
         for p in range(2):
             i = place[1 - p]
             copies = second[job, p]
             for k, j, half, to in ((0, up(i), 0, plus[1 - p]), (1, up(i, 3), 1, minus[1 - p])):
                 copies[k].wait_recv()
                 target = piece(job, p, j, half)
-                target[...] = target[...] + rel2[job, p, k, :, :n]
+                target[...] = target[...] + rel2[at, p, k, cut[0], columns]
                 copies.append(
                     remote(
-                        target, fin2.at[job, p, k, pl.ds(16 * half, 16), width],
+                        target, fin2.at[at, p, k, cut[half], columns],
                         s2_s.at[job, p, 4 + k], s2_r.at[job, p, 4 + k], to,
                     )
                 )
@@ -293,31 +428,38 @@
     third = {}
 
     def ring_cross(job):
-        slot, n = job % 2, WIDTHS[job]
-        width = pl.ds(0, n)
+        _, columns, rows, deep = block_of(job)
+        at = min(job, 3)
         for p in range(2):
             for k in (2, 3, 4, 5):
                 second[job, p][k].wait_recv()
-            mine = piece(job, p, place[1 - p])
-            mine[...] = mine[...] + fin2[job, p, 0, :, :n] + fin2[job, p, 1, :, :n]
-        third[job] = remote(
-            grads.at[slot, y, z, 1 - l, :, width], last.at[job, :, width], s3_s.at[job], s3_r.at[job], across
-        )
+            total = (
+                piece(job, p, place[1 - p])[...]
+                + fin2[at, p, 0, rows, columns]
+                + fin2[at, p, 1, rows, columns]
+            )
+            if deep == 32:
+                fin2[at, p, 0, :, columns] = total
+            else:
+                o_out[p * deep : (p + 1) * deep] = total
+        if deep == 32:
+            third[job] = remote(
+                fin2.at[at, 1 - l, 0, :, columns], last.at[at, :, columns], s3_s.at[job], s3_r.at[job], across
+            )
 
     def ring_end(job):
-        slot, n = job % 2, WIDTHS[job]
+        columns = block_of(job)[1]
         third[job].wait()
-        total = grads[slot, y, z, l, :, :n] + last[job, :, :n]
+        total = fin2[job, l, 0, :, columns] + last[job, :, columns]
         if job < 3:
             (o_down, o_gate, o_up)[job][...] = total
         else:
             for j in range(3):
                 o_in[j] = total[:, j * CH : (j + 1) * CH]
-            o_out[...] = total[:, 3 * CH :]
-
-    def ring_sent(job):
-        for p in range(2):
-            for copy in first[job, p] + second[job, p]:
+
+    def ring_sent(job, copies):
+        for p in range(2):
+            for copy in copies[job, p]:
                 copy.wait_send()
 
     back = {}
@@ -335,13 +477,15 @@
                 - m * (scale * scale * scale) * jnp.mean(weighted * m, axis=-1, keepdims=True)
             )
             cot[r] = total
-            gbr[rows] = total.astype(BF16)
-        gmix = mm(gbr[rows_of(g)], wout[...], NN)
+            gf[rows] = total.astype(BF16)
+        gmix = mm(gf[rows_of(g)], wout[...], NN)
         for k in range(2):
             r = 2 * g + k
             rows = pl.ds(r * TB, TB)
             value = gmix[k * TB : (k + 1) * TB]
-            gproj[1, rows] = (value * conv[rows]).astype(BF16)
+            total = conv(r, 0, TB)
+            gg[rows, CH : 2 * CH] = (value * total).astype(BF16)
+            wg[rows, 0:CH] = (proj[1, rows] * total).astype(BF16)
             gce[r, 0:TB] = value * proj[1, rows]
             sbuf[r] = gce[r, 0:8] * keep[r]
             back[r] = remote(sbuf.at[r], hb.at[r], h_s.at[1, r], h_r.at[1, r], previous)
@@ -357,11 +501,11 @@
                     value * bxe[r, 6 + k : 6 + k + TB], axis=0, keepdims=True
                 )
             gbx = w_conv[2:3] * value + w_conv[1:2] * gce[r, 1 : 1 + TB] + w_conv[0:1] * gce[r, 2 : 2 + TB]
-            gproj[0, rows] = (gbx * proj[2, rows]).astype(BF16)
-            gproj[2, rows] = (gbx * proj[0, rows]).astype(BF16)
-        partial = mm(gproj[0, rows_of(g)], win[0], NT)
+            gg[rows, 0:CH] = (gbx * proj[2, rows]).astype(BF16)
+            gg[rows, 2 * CH : 3 * CH] = (gbx * proj[0, rows]).astype(BF16)
+        partial = mm(gg[rows_of(g), 0:CH], win[0], NT)
         for j in (1, 2):
-            partial += mm(gproj[j, rows_of(g)], win[j], NT)
+            partial += mm(gg[rows_of(g), j * CH : (j + 1) * CH], win[j], NT)
         for k in range(2):
             part[0, 2 * g + k] = partial[k * TB : (k + 1) * TB]
             sum_begin(2, 2 * g + k)
@@ -414,113 +558,158 @@
             total += ar[stage, k]
         small[...] = total
 
+    loads["wout"].wait()
+    weight_begin()
+    pl.semaphore_wait(barrier, len(partners))
+    weight_far()
     loads["tok"].wait()
     loads["win"].wait()
     mixer_in(0)
+    send_halo(0)
+    mixer_out(0)
     mixer_in(1)
-    pl.semaphore_wait(barrier, len(partners))
-    send_halo(0)
     send_halo(1)
-    loads["wout"].wait()
-    mixer_out(0)
     mixer_out(1)
-    for r in range(4):
-        sum_cross(0, r)
+    weight_first()
     loads["cot"].wait()
     loads["wd"].wait()
     grad_hidden(0)
     grad_hidden(1)
+    weight_second()
+    mixer_edge()
+    mix_pass(0)
+    mix_pass(1)
+    mix_pass(2)
+    weight_third()
+    mix_pass(3)
+    mix_pass(4)
     loads["wg"].wait()
     loads["wu"].wait()
-    sum_share(0, 0)
-    sum_share(0, 1)
-    sum_end(0, 0)
-    sum_end(0, 1)
+    weight_end()
+    mix_end(0)
+    mix_end(1)
+    mix_end(4)
+    branch(0)
     ffn(0)
-    ffn_back(0)
-    sum_share(0, 2)
-    sum_share(0, 3)
-    sum_cross(1, 0)
-    sum_cross(1, 1)
-    sum_end(0, 2)
-    sum_end(0, 3)
+    mix_end(2)
+    mix_end(3)
+    branch(1)
     ffn(1)
     product(0, gf, hid[...], 0, HID)
     ring_begin(0)
+    ffn_back(0)
     ffn_back(1)
-    sum_cross(1, 2)
-    sum_cross(1, 3)
+    for r in range(4):
+        sum_cross(1, r)
     product(1, aff, gg[...], 0, HID)
+    ring_relay(0)
     ring_begin(1)
     sum_share(1, 0)
     sum_share(1, 1)
     sum_end(1, 0)
     sum_end(1, 1)
     mixer_back(0)
-    mixer_back_in(0)
-    sum_cross(2, 0)
-    sum_cross(2, 1)
-    ring_relay(0)
+    ring_turn(0)
+    ring_sent(0, first)
+    product(0, aff, gu[...], 0, HID)
+    ffn_out(0)
     sum_share(1, 2)
+    sum_cross(3, 0)
+    sum_cross(3, 1)
+    ring_relay(1)
+    ring_begin(2)
     sum_share(1, 3)
     sum_end(1, 2)
     sum_end(1, 3)
     mixer_back(1)
+    product(None, gf, wg[0:POS, 0:CH], 0, CH)
+    pair_begin()
+    mixer_back_in(0)
+    ffn_out(1)
+    sum_cross(2, 0)
+    sum_cross(2, 1)
+    ring_relay_two(0)
     mixer_back_in(1)
+    ring_turn(1)
+    ring_sent(1, first)
     sum_cross(2, 2)
     sum_cross(2, 3)
-    ring_turn(0)
-    ffn_out(0)
-    ffn_out(1)
-    ring_relay_two(0)
-    ring_relay(1)
-    for r in range(4):
-        sum_cross(3, r)
+    for g in (0, 1):
+        aff[rows_of(g)] = normed(g)
+    product(1, aff, gg[:, 0 : 3 * CH], 0, 3 * CH)
+    ring_relay(2)
+    ring_begin(3)
+    pair_end()
+    ring_begin(4)
     ring_cross(0)
-    ring_end(0)
-    ring_sent(0)
-    product(0, aff, gu[...], 0, HID)
-    ring_begin(2)
-    for r in range(4):
-        sum_share(2, r)
-    for r in range(4):
+    ring_relay_two(1)
+    sum_share(3, 0)
+    sum_share(3, 1)
+    sum_cross(3, 2)
+    sum_cross(3, 3)
+    sum_share(2, 0)
+    ring_sent(0, second)
+    ring_relay(3)
+    ring_relay(4)
+    sum_share(2, 1)
+    for r in (0, 1):
+        sum_end(3, r)
+        result_out(r)
+        sum_end(2, r)
+        tokens_out(r)
+    ring_cross(1)
+    ring_sent(1, second)
+    ring_turn(2)
+    sum_share(2, 2)
+    ring_relay_two(2)
+    ring_turn(3)
+    ring_turn(4)
+    sum_share(2, 3)
+    for r in (2, 3):
         sum_end(2, r)
         tokens_out(r)
     small_begin(0)
-    ring_turn(1)
+    ring_cross(2)
+    ring_relay_two(3)
+    ring_relay_two(4)
     small_end(0)
     small_begin(1)
-    ring_relay_two(1)
+    ring_end(0)
+    ring_end(1)
+    ring_cross(3)
+    ring_cross(4)
     small_end(1)
     small_begin(2)
-    ring_cross(1)
-    ring_end(1)
-    small_end(2)
-    ring_sent(1)
-    for j in range(3):
-        product(1, act_in, gproj[j], j * CH, CH)
-    product(1, gbr, amix[...], 3 * CH, CH)
-    ring_begin(3)
-    o_small[...] = small[...]
-    ring_relay(2)
-    for r in range(4):
-        sum_share(3, r)
-    for r in range(4):
+    sum_share(3, 2)
+    sum_share(3, 3)
+    for r in (2, 3):
         sum_end(3, r)
         result_out(r)
-    ring_turn(2)
-    ring_relay_two(2)
-    ring_relay(3)
-    ring_cross(2)
-    ring_turn(3)
     ring_end(2)
-    ring_relay_two(3)
-    ring_sent(2)
-    ring_cross(3)
+    small_end(2)
+    o_small[...] = small[...]
+    for job in range(5):
+        if job >= 2:
+            ring_sent(job, first)
+            ring_sent(job, second)
     ring_end(3)
-    ring_sent(3)
     for copy in outs:
         copy.wait()
+
+
+def finish(*refs):
+    ins, outs = refs[:8], refs[8:]
+    outs[0][...] = ins[0][...]
+    outs[1][...] = ins[1][...]
+
+    @pl.when(pl.program_id(0) == 0)
+    def _():
+        for src, dst in zip(ins[2:7], outs[2:7]):
+            dst[...] = src[...]
+        small = ins[7]
+        outs[7][...] = small[1]
+        outs[8][...] = small[0]
+        outs[9][...] = small[2:5, 0:CH]
 
 
 def on_device(
@@ -552,12 +741,9 @@
             pltpu.VMEM((D, HID), BF16),
             pltpu.VMEM((D, HID), BF16),
             pltpu.VMEM((D, HID), BF16),
-            pltpu.VMEM((POS, D), BF16),
             pltpu.VMEM((3, POS, CH), F32),
             pltpu.VMEM((ROWS, TB + 8, CH), F32),
             pltpu.VMEM((ROWS, TB + 8, CH), F32),
-            pltpu.VMEM((POS, CH), F32),
-            pltpu.VMEM((POS, CH), BF16),
             pltpu.VMEM((ROWS, TB, D), F32),
             pltpu.VMEM((POS, D), BF16),
             pltpu.VMEM((POS, HID), BF16),
@@ -565,9 +751,7 @@
             pltpu.VMEM((POS, HID), BF16),
             pltpu.VMEM((POS, D), BF16),
             pltpu.VMEM((POS, HID), F32),
-            pltpu.VMEM((POS, D), BF16),
-            pltpu.VMEM((3, POS, CH), BF16),
-            pltpu.VMEM((ROWS, 8, CH), F32),
+                pltpu.VMEM((ROWS, 8, CH), F32),
             pltpu.VMEM((ROWS, 8, CH), F32),
             pltpu.VMEM((ROWS, 8, CH), F32),
             pltpu.VMEM((2, ROWS, TB, D), F32),
@@ -580,10 +764,16 @@
             pltpu.VMEM((4, 2, 2, 16, HID), F32),
             pltpu.VMEM((4, 2, 2, 32, HID), F32),
             pltpu.VMEM((4, 32, HID), F32),
+            pltpu.VMEM((4, 4, 2, 32, CH), F32),
+            pltpu.VMEM((4, 4, 32, CH), F32),
             pltpu.VMEM((8, D), F32),
             pltpu.VMEM((3, 4, 8, D), F32),
             dma((7,)),
             dma((8,)),
+            dma((3, 5)),
+            dma((3, 5)),
+            dma((22,)),
+            dma((22,)),
             dma((2, 4)),
             dma((2, 4)),
             dma((4, 4)),
@@ -592,12 +782,14 @@
             dma((4, 4)),
             dma((4, 4)),
             dma((4, 4)),
-            dma((4, 2, 6)),
-            dma((4, 2, 6)),
-            dma((4, 2, 6)),
-            dma((4, 2, 6)),
+            dma((5, 2, 6)),
+            dma((5, 2, 6)),
+            dma((5, 2, 6)),
+            dma((5, 2, 6)),
             dma((4,)),
             dma((4,)),
+            dma((1,)),
+            dma((1,)),
             dma((3, 3)),
             dma((3, 4)),
             pltpu.SemaphoreType.REGULAR((2, 2, 2)),
@@ -607,13 +799,34 @@
         ),
         name="block",
     )(
-        start_flags, tokens, cotangent, w_in, w_out, w_gate, w_up, w_down,
+        start_flags.T, tokens, cotangent, w_in, w_out, w_gate, w_up, w_down,
         norm_one.reshape(1, D), norm_two.reshape(1, D), w_conv,
     )
-    result, grad_tokens, g_in, g_out, g_gate, g_up, g_down, g_small = outs
-    return (
-        result, grad_tokens, g_small[1], g_in, g_small[2:5, :CH], g_out, g_small[0], g_gate, g_up, g_down,
-    )
+    row = pl.BlockSpec((1, TB, D), lambda r: (r, 0, 0))
+
+    def whole(array):
+        return pl.BlockSpec(array.shape, lambda r: (0,) * array.ndim)
+
+    result, grad_tokens, g_in, g_out, g_gate, g_up, g_down, one, two, taps = pl.pallas_call(
+        finish,
+        out_shape=tuple(shape(o.shape, F32) for o in outs[:2])
+        + (
+            shape((3, 32, CH), F32),
+            shape((32, CH), F32),
+            shape((32, HID), F32),
+            shape((32, HID), F32),
+            shape((32, HID), F32),
+            shape((D,), F32),
+            shape((D,), F32),
+            shape((3, CH), F32),
+        ),
+        grid=(ROWS,),
+        in_specs=[row, row] + [whole(o) for o in outs[2:]],
+        out_specs=(row, row) + tuple(whole(o) for o in outs[2:7])
+        + (pl.BlockSpec((D,), lambda r: (0,)),) * 2 + (pl.BlockSpec((3, CH), lambda r: (0, 0)),),
+        name="finish",
+    )(*outs)
+    return result, grad_tokens, one, g_in, taps, g_out, two, g_gate, g_up, g_down
 
 
 def solution(mesh):

time: 219 us -> 147 us (0.67)
  Pallas kernels: 206 us -> 144 us
  local copies, waits for them, and re-layouts: 11.9 us -> 0 us
    pallas_call x1, Pallas kernels: 206 us -> 139 us  [on_device(): pl.pallas_call(kernel, out_shape=(shape((ROWS, TB, D), F32), shape((ROWS,...]
    unnamed x20 -> x0, local copies, waits for them, and re-layouts: 9.2 us -> none
    pallas_call x0 -> x1, Pallas kernels: none -> 5.11 us  [on_device(): pl.pallas_call(finish, out_shape=tuple((shape(o.shape, F32) for o in outs...]
    slice x2 -> x0, local copies, waits for them, and re-layouts: 2.73 us -> none  [the longest x1 1.43 us: on_device(): g_small[0]]
where the time goes in v2:
time: 147 us; the launch traced here: 145 us
  Pallas kernels  144 us (98%)
    pallas_call x1, Pallas kernels, on_device(): pl.pallas_call(kernel, out_shape=(shape((ROWS, TB, D), F32), shape((ROWS,...  139 us
    pallas_call x1, Pallas kernels, on_device(): pl.pallas_call(finish, out_shape=tuple((shape(o.shape, F32) for o in outs...  5.11 us

profile of v2, /device:TPU:0, one launch (start us, length us, event | category | flops | bytes accessed | tf_op | source)
XLA Modules:
  0.0 145.0 jit_solution(6194640799156747559)
XLA Ops:
  0.6 139.1 %block.1 = (f32[4,128,1024]{2,1,0:T(8,128)}, f32[4,128,1024]{2,1,0:T(8,128)}, f32[3,32,256]{2,1,0:T(8,128)}, f32[32,256]{1,0:T(8,128)}, f32[32,1152]{1,0:T(8,128...) custom-call(s32[1,4]{1,0:T(1,128)} %bitcast.5, f32[4,128,1024]{2,1,0:T(8,128)} %tokens.1, ...), custom_call_target="tpu_custom_call" | custom-call | tf_op jit(solution)/shard_map/block/pallas_call | solution.py:722
  139.7 5.1 %finish.1 = (f32[4,128,1024]{2,1,0:T(8,128)}, f32[4,128,1024]{2,1,0:T(8,128)}, f32[3,32,256]{2,1,0:T(8,128)}, f32[32,256]{1,0:T(8,128)}, f32[32,1152]{1,0:T(8,12...) custom-call(f32[4,128,1024]{2,1,0:T(8,128)} %get-tuple-element.28.refs_0_, ...), custom_call_target="tpu_custom_call" | custom-call | tf_op jit(solution)/shard_map/finish/pallas_call | solution.py:810

commit v3 on v2

--- a/solution.py
+++ b/solution.py
@@ -40,7 +40,7 @@
     part, c_recv, x_recv, a_recv,
     grads, rel1, fin1, rel2, fin2, last, grads_out, paired, small, ar,
     in_sem, out_sem, m_s, m_r, v_s, v_r, h_s, h_r, c_s, c_r, x_s, x_r, a_s, a_r,
-    s1_s, s1_r, s2_s, s2_r, s3_s, s3_r, p_s, p_r, ar_s, ar_r, credit,
+    s1_s, s1_r, split_s, split_r, s2_s, s2_r, s3_s, s3_r, p_s, p_r, ar_s, ar_r, credit,
 ):
     s = lax.axis_index("seq")
     w = lax.axis_index("wt")
@@ -111,9 +111,8 @@
         for k in range(2):
             bxe[2 * g + k, 8:] = bx[k * TB : (k + 1) * TB]
 
-    def send_halo(g):
-        for r in (2 * g, 2 * g + 1):
-            halo[r] = remote(bxe.at[r, pl.ds(TB, 8)], hf.at[r], h_s.at[0, r], h_r.at[0, r], following)
+    def send_halo():
+        halo[0] = remote(bxe.at[:, pl.ds(TB, 8)], hf, h_s.at[2], h_r.at[2], following)
 
     mine = pl.ds(pl.multiple_of(w * CH, CH), CH)
     theirs = pl.ds(pl.multiple_of(((1 - h) * 2 + c) * CH, CH), CH)
@@ -170,8 +169,10 @@
                 weight["second", p, k].wait_recv()
                 weight_pass(p, k)
 
+    def weight_near():
+        weight["mate"].wait()
+
     def weight_end():
-        weight["mate"].wait()
         weight["far"].wait_send()
         for p in range(2):
             for k in (1, 2, 3):
@@ -183,8 +184,8 @@
     mix = {}
 
     def mix_block(k, columns):
-        if k < 4:
-            return part.at[0, k, pl.ds(8, TB - 8), columns]
+        if k < 2:
+            return part.at[0, pl.ds(2 * k, 2), pl.ds(8, TB - 8), columns]
         return part.at[0, :, pl.ds(0, 8), columns]
 
     def mix_send(k):
@@ -197,9 +198,11 @@
         block = mix_block(k, theirs)
         mix["pass", k] = remote(block, block, m_s.at[2, k], m_r.at[2, k], mate)
 
+    def mix_near(k):
+        mix["mate", k].wait()
+
     def mix_end(k):
         mix["far", k].wait_send()
-        mix["mate", k].wait()
         mix["pass", k].wait()
 
     def conv(r, at, count):
@@ -217,67 +220,70 @@
     def mixer_out(g):
         for r in (2 * g, 2 * g + 1):
             taps(r, 8, TB - 8)
-            mix_send(r)
+        mix_send(g)
 
     def mixer_edge():
+        halo[0].wait()
         for r in range(4):
-            halo[r].wait()
             bxe[r, 0:8] = hf[r] * keep[r]
             taps(r, 0, 8)
-        mix_send(4)
-
-    def branch(g):
-        left = part[0, 2 * g : 2 * g + 2].reshape(2 * TB, D).astype(BF16)
+        mix_send(2)
+
+    def branch(chip, start):
+        half = pl.ds(pl.multiple_of(chip * 2 * CH, 2 * CH), 2 * CH)
+        left = part[0, :, :, half].reshape(POS, 2 * CH).astype(BF16)
         for i in range(4):
-            right = grads[1, i, :, :, :, 0:D].reshape(256, D).astype(BF16)
-            value = mm(left, right, NT).reshape(2, TB, 256)
+            right = grads[1, i, :, :, :, half].reshape(256, 2 * CH).astype(BF16)
             columns = pl.ds(i * 256, 256)
-            mid[2 * g : 2 * g + 2, :, columns] = tok[2 * g : 2 * g + 2, :, columns] + value
+            mid[:, :, columns] = start[:, :, columns] + mm(left, right, NT).reshape(ROWS, TB, 256)
 
     csend, xsend, asend = {}, {}, {}
     own = pl.ds(pl.multiple_of(c * HALF, HALF), HALF)
     other = pl.ds(pl.multiple_of((1 - c) * HALF, HALF), HALF)
     bank_of = (None, 1, 0, 1)
 
-    def sum_begin(q, r):
-        b = bank_of[q]
-        csend[q, r] = remote(part.at[b, r, other], c_recv.at[b, r], c_s.at[q, r], c_r.at[q, r], mate)
-
-    def sum_cross(q, r):
-        b = bank_of[q]
-        csend[q, r].wait_recv()
-        part[b, r, own] = part[b, r, own] + c_recv[b, r]
-        xsend[q, r] = remote(part.at[b, r, own], x_recv.at[q - 1, r], x_s.at[q, r], x_r.at[q, r], far)
-
-    def sum_share(q, r):
-        b = bank_of[q]
-        xsend[q, r].wait()
-        part[b, r, own] = part[b, r, own] + x_recv[q - 1, r]
-        asend[q, r] = remote(part.at[b, r, own], a_recv.at[b, r], a_s.at[q, r], a_r.at[q, r], mate)
-
-    def sum_end(q, r):
-        b = bank_of[q]
-        csend[q, r].wait_send()
-        asend[q, r].wait()
-        part[b, r, other] = a_recv[b, r]
+    def sum_begin(q, g):
+        b, two = bank_of[q], pl.ds(2 * g, 2)
+        csend[q, g] = remote(part.at[b, two, other], c_recv.at[b, two], c_s.at[b, g], c_r.at[q - 1, g], mate)
+
+    def sum_cross(q, g):
+        b, two = bank_of[q], pl.ds(2 * g, 2)
+        csend[q, g].wait_recv()
+        part[b, two, own] = part[b, two, own] + c_recv[b, two]
+        xsend[q, g] = remote(part.at[b, two, own], x_recv.at[q - 1, two], x_s.at[b, g], x_r.at[q - 1, g], far)
+
+    def sum_share(q, g):
+        b, two = bank_of[q], pl.ds(2 * g, 2)
+        xsend[q, g].wait()
+        part[b, two, own] = part[b, two, own] + x_recv[q - 1, two]
+        asend[q, g] = remote(part.at[b, two, own], a_recv.at[b, two], a_s.at[b, g], a_r.at[q - 1, g], mate)
+
+    def sum_end(q, g):
+        b, two = bank_of[q], pl.ds(2 * g, 2)
+        csend[q, g].wait_send()
+        asend[q, g].wait()
+        part[b, two, other] = a_recv[b, two]
 
     def grad_hidden(g):
-        value = cot[2 * g : 2 * g + 2].reshape(2 * TB, D).astype(BF16)
-        gf[rows_of(g)] = value
+        whole = cot[2 * g : 2 * g + 2].reshape(2 * TB, D)
+        value = whole.astype(BF16)
+        for i in range(2):
+            gf[i, :, g * 256 : (g + 1) * 256] = whole[:, i * POS : (i + 1) * POS].T.astype(BF16)
         for n, width in TILES:
             gh[rows_of(g), n : n + width] = mm(value, wd[:, n : n + width], NN)
 
-    def ffn(g):
-        for r in (2 * g, 2 * g + 1):
-            rows = pl.ds(r * TB, TB)
+    def ffn_norm():
+        for r in range(ROWS):
             m = mid[r]
             scale = lax.rsqrt(jnp.mean(m * m, axis=-1, keepdims=True) + EPS)
-            aff[rows] = (m * scale * norm_two[...]).astype(BF16)
-        act = aff[rows_of(g)]
-        for n, width in TILES:
-            at = (rows_of(g), pl.ds(n, width))
-            gate = mm(act, wg[:, n : n + width], NN)
-            upv = mm(act, wu[:, n : n + width], NN)
+            aff[r * TB : (r + 1) * TB] = (m * scale * norm_two[...]).astype(BF16)
+
+    def ffn_tiles(tiles):
+        act = aff[...]
+        for n, width in tiles:
+            at = (slice(None), slice(n, n + width))
+            gate = mm(act, wg[at], NN)
+            upv = mm(act, wu[at], NN)
             sig = jax.nn.sigmoid(gate)
             silu = gate * sig
             grad = gh[at]
@@ -287,15 +293,13 @@
 
     def ffn_back(g):
         partial = mm(gg[rows_of(g)], wg[...], NT) + mm(gu[rows_of(g)], wu[...], NT)
-        for k in range(2):
-            part[1, 2 * g + k] = partial[k * TB : (k + 1) * TB]
-            sum_begin(1, 2 * g + k)
+        part[1, 2 * g : 2 * g + 2] = partial.reshape(2, TB, D)
+        sum_begin(1, g)
 
     def ffn_out(g):
         partial = mm(hid[rows_of(g)], wd[...], NT)
-        for k in range(2):
-            part[1, 2 * g + k] = partial[k * TB : (k + 1) * TB]
-            sum_begin(3, 2 * g + k)
+        part[1, 2 * g : 2 * g + 2] = partial.reshape(2, TB, D)
+        sum_begin(3, g)
 
     def product(slot, left, right, n, width):
         @pl.loop(0, 4)
@@ -303,19 +307,44 @@
             columns = pl.ds(pl.multiple_of(i * 256, 256), 256)
             value = mm(left[:, columns], right, TN)
             value = value.reshape(4, 2, 32, width)
-            if slot is None:
-                grads_out[i] = value
-            else:
-                grads[slot, i, :, :, :, n : n + width] = value
+            grads[slot, i, :, :, :, n : n + width] = value
+
+    def product_down(tiles):
+        for n, width in tiles:
+            right = hid[:, n : n + width]
+            for i in range(2):
+                value = mm(gf[i], right, NN).reshape(2, 4, 2, 32, width)
+                grads[0, 2 * i : 2 * i + 2, :, :, :, n : n + width] = value
+
+    def product_out():
+        right = wg[0:POS, 0:CH]
+        for i in range(4):
+            left = gf[i // 2, :, i % 2 * 256 : (i % 2 + 1) * 256]
+            grads_out[i] = mm(left, right, TN).reshape(4, 2, 32, CH)
+
+    outs = []
+
+    def leave(src, dst):
+        outs.append(pltpu.make_async_copy(src, dst, out_sem.at[len(outs)]))
+        outs[-1].start()
 
     place = (y, z)
+
+    def slot_of(job):
+        return 2 if job == 4 else job % 2
 
     def block_of(job):
         slot, at, n, deep = JOBS[job]
         return slot, pl.ds(at, n), pl.ds(0, deep), deep
 
-    def chunk(job, p, j, half=None):
-        slot, columns, rows, deep = block_of(job)
+    def sems_of(job, p, k):
+        if k >= 6:
+            return split_s.at[p, k - 6], split_r.at[p, k - 6]
+        return s1_s.at[slot_of(job), p, k], s1_r.at[slot_of(job), p, k]
+
+    def chunk(job, p, j, half=None, columns=None):
+        slot, every, rows, deep = block_of(job)
+        columns = every if columns is None else columns
         cut = pl.ds(0, 4) if half is None else pl.ds(2 * half, 2)
         if deep != 32:
             rows = pl.ds(deep * p, deep)
@@ -338,21 +367,32 @@
 
     first = {}
 
-    def ring_begin(job):
+    def ring_begin(job, cut=None):
         slot, columns, rows, _ = block_of(job)
+        columns, base = (columns, 0) if cut is None else (pl.ds(*cut), 6 if cut[0] else 0)
         for p in range(2):
             i = place[p]
             if job in (2, 3):
                 pl.semaphore_wait(credit.at[slot, p, 0], 1)
                 pl.semaphore_wait(credit.at[slot, p, 1], 1)
-            sems = lambda k: (s1_s.at[job, p, k], s1_r.at[job, p, k])
-            a, b = plus[p], minus[p]
-            first[job, p] = [
-                remote(chunk(job, p, up(i, 2), 0), rel1.at[slot, p, 0, :, rows, columns], *sems(0), a),
-                remote(chunk(job, p, up(i, 2), 1), rel1.at[slot, p, 1, :, rows, columns], *sems(1), b),
-                remote(chunk(job, p, up(i), 1), fin1.at[slot, p, 0, pl.ds(2, 2), rows, columns], *sems(2), a),
-                remote(chunk(job, p, up(i, 3), 0), fin1.at[slot, p, 1, pl.ds(0, 2), rows, columns], *sems(3), b),
-            ]
+            copies = first.setdefault((job, p), {})
+            for k, half, to in ((0, 0, plus[p]), (1, 1, minus[p])):
+                copies[base + k] = remote(
+                    chunk(job, p, up(i, 2), half, columns), rel1.at[slot, p, k, :, rows, columns],
+                    *sems_of(job, p, base + k), to,
+                )
+
+    def ring_fill(job, cut=None):
+        slot, columns, rows, _ = block_of(job)
+        columns, base = (columns, 2) if cut is None else (pl.ds(*cut), 8 if cut[0] else 2)
+        for p in range(2):
+            i = place[p]
+            for k, half, to in ((0, 1, plus[p]), (1, 0, minus[p])):
+                first[job, p][base + k] = remote(
+                    chunk(job, p, up(i, 1 + 2 * k), half, columns),
+                    fin1.at[slot, p, k, pl.ds(2 * half, 2), rows, columns],
+                    *sems_of(job, p, base + k), to,
+                )
 
     def ring_relay(job):
         slot, columns, rows, _ = block_of(job)
@@ -361,14 +401,14 @@
             copies = first[job, p]
             for k, j, half, to in ((0, up(i), 0, plus[p]), (1, up(i, 3), 1, minus[p])):
                 copies[k].wait_recv()
+                if 6 + k in copies:
+                    copies[6 + k].wait_recv()
                 target = chunk(job, p, j, half)
                 for m in range(2):
                     target[m] = target[m] + rel1[slot, p, k, m, rows, columns]
-                copies.append(
-                    remote(
-                        target, fin1.at[slot, p, k, pl.ds(2 * half, 2), rows, columns],
-                        s1_s.at[job, p, 4 + k], s1_r.at[job, p, 4 + k], to,
-                    )
+                copies[4 + k] = remote(
+                    target, fin1.at[slot, p, k, pl.ds(2 * half, 2), rows, columns],
+                    s1_s.at[slot_of(job), p, 4 + k], s1_r.at[slot_of(job), p, 4 + k], to,
                 )
 
     second = {}
@@ -384,8 +424,9 @@
         slot, columns, rows, deep = block_of(job)
         at, cut = min(job, 3), (pl.ds(0, deep // 2), pl.ds(deep // 2, deep // 2))
         for p in range(2):
-            for k in (2, 3, 4, 5):
-                first[job, p][k].wait_recv()
+            for k in (2, 3, 8, 9, 4, 5):
+                if k in first[job, p]:
+                    first[job, p][k].wait_recv()
             mine = chunk(job, p, place[p])
 
             @pl.loop(0, 4)
@@ -399,14 +440,23 @@
                 pl.semaphore_signal(credit.at[slot, p, 0], inc=1, device_id=minus[p], device_id_type=MESH)
                 pl.semaphore_signal(credit.at[slot, p, 1], inc=1, device_id=plus[p], device_id_type=MESH)
             i = place[1 - p]
-            sems = lambda k: (s2_s.at[job, p, k], s2_r.at[job, p, k])
+            sems = lambda k: (s2_s.at[slot_of(job), p, k], s2_r.at[job, p, k])
             a, b = plus[1 - p], minus[1 - p]
-            second[job, p] = [
-                remote(piece(job, p, up(i, 2), 0), rel2.at[at, p, 0, cut[0], columns], *sems(0), a),
-                remote(piece(job, p, up(i, 2), 1), rel2.at[at, p, 1, cut[0], columns], *sems(1), b),
-                remote(piece(job, p, up(i), 1), fin2.at[at, p, 0, cut[1], columns], *sems(2), a),
-                remote(piece(job, p, up(i, 3), 0), fin2.at[at, p, 1, cut[0], columns], *sems(3), b),
-            ]
+            if job >= 3:
+                beyond = dev(z=up(z, 2)) if p == 0 else dev(y=up(y, 2))
+                second[job, p] = {
+                    0: remote(piece(job, p, up(i, 2), 0), rel2.at[at, p, 0, cut[0], columns], *sems(0), beyond),
+                    1: remote(piece(job, p, up(i, 2), 1), rel2.at[at, p, 1, cut[0], columns], *sems(1), beyond),
+                    2: remote(piece(job, p, up(i)), fin2.at[at, p, 0, rows, columns], *sems(2), a),
+                    3: remote(piece(job, p, up(i, 3)), fin2.at[at, p, 1, rows, columns], *sems(3), b),
+                }
+                continue
+            second[job, p] = {
+                0: remote(piece(job, p, up(i, 2), 0), rel2.at[at, p, 0, cut[0], columns], *sems(0), a),
+                1: remote(piece(job, p, up(i, 2), 1), rel2.at[at, p, 1, cut[0], columns], *sems(1), b),
+                2: remote(piece(job, p, up(i), 1), fin2.at[at, p, 0, cut[1], columns], *sems(2), a),
+                3: remote(piece(job, p, up(i, 3), 0), fin2.at[at, p, 1, cut[0], columns], *sems(3), b),
+            }
 
     def ring_relay_two(job):
         _, columns, _, deep = block_of(job)
@@ -418,11 +468,9 @@
                 copies[k].wait_recv()
                 target = piece(job, p, j, half)
                 target[...] = target[...] + rel2[at, p, k, cut[0], columns]
-                copies.append(
-                    remote(
-                        target, fin2.at[at, p, k, cut[half], columns],
-                        s2_s.at[job, p, 4 + k], s2_r.at[job, p, 4 + k], to,
-                    )
+                copies[4 + k] = remote(
+                    target, fin2.at[at, p, k, cut[half], columns],
+                    s2_s.at[slot_of(job), p, 4 + k], s2_r.at[job, p, 4 + k], to,
                 )
 
     third = {}
@@ -431,18 +479,23 @@
         _, columns, rows, deep = block_of(job)
         at = min(job, 3)
         for p in range(2):
-            for k in (2, 3, 4, 5):
+            for k in (2, 3, 0, 1) if job >= 3 else (2, 3, 4, 5):
                 second[job, p][k].wait_recv()
             total = (
                 piece(job, p, place[1 - p])[...]
                 + fin2[at, p, 0, rows, columns]
                 + fin2[at, p, 1, rows, columns]
             )
+            if job >= 3:
+                low = pl.ds(0, deep // 2)
+                total += jnp.concatenate([rel2[at, p, 0, low, columns], rel2[at, p, 1, low, columns]], axis=0)
             if deep == 32:
                 fin2[at, p, 0, :, columns] = total
             else:
-                o_out[p * deep : (p + 1) * deep] = total
-        if deep == 32:
+                paired[0, 0, p * deep : (p + 1) * deep] = total
+        if deep != 32:
+            leave(paired.at[0, 0], o_out)
+        else:
             third[job] = remote(
                 fin2.at[at, 1 - l, 0, :, columns], last.at[at, :, columns], s3_s.at[job], s3_r.at[job], across
             )
@@ -450,16 +503,16 @@
     def ring_end(job):
         columns = block_of(job)[1]
         third[job].wait()
-        total = fin2[job, l, 0, :, columns] + last[job, :, columns]
+        last[job, :, columns] = fin2[job, l, 0, :, columns] + last[job, :, columns]
         if job < 3:
-            (o_down, o_gate, o_up)[job][...] = total
+            leave(last.at[job], (o_down, o_gate, o_up)[job])
         else:
             for j in range(3):
-                o_in[j] = total[:, j * CH : (j + 1) * CH]
+                leave(last.at[job, :, pl.ds(j * CH, CH)], o_in.at[j])
 
     def ring_sent(job, copies):
         for p in range(2):
-            for copy in copies[job, p]:
+            for copy in copies[job, p].values():
                 copy.wait_send()
 
     back = {}
@@ -477,8 +530,9 @@
                 - m * (scale * scale * scale) * jnp.mean(weighted * m, axis=-1, keepdims=True)
             )
             cot[r] = total
-            gf[rows] = total.astype(BF16)
-        gmix = mm(gf[rows_of(g)], wout[...], NN)
+            for i in range(2):
+                gf[i, rows] = total[:, i * POS : (i + 1) * POS].astype(BF16)
+        gmix = mm(gf[0, rows_of(g)], wout[0:POS], NN) + mm(gf[1, rows_of(g)], wout[POS:], NN)
         for k in range(2):
             r = 2 * g + k
             rows = pl.ds(r * TB, TB)
@@ -488,12 +542,13 @@
             wg[rows, 0:CH] = (proj[1, rows] * total).astype(BF16)
             gce[r, 0:TB] = value * proj[1, rows]
             sbuf[r] = gce[r, 0:8] * keep[r]
-            back[r] = remote(sbuf.at[r], hb.at[r], h_s.at[1, r], h_r.at[1, r], previous)
+        two = pl.ds(2 * g, 2)
+        back[g] = remote(sbuf.at[two], hb.at[two], h_s.at[g], h_r.at[g], previous)
 
     def mixer_back_in(g):
+        back[g].wait()
         for r in (2 * g, 2 * g + 1):
             rows = pl.ds(r * TB, TB)
-            back[r].wait()
             gce[r, TB:] = hb[r]
             value = gce[r, 0:TB]
             for k in range(3):
@@ -506,11 +561,8 @@
         partial = mm(gg[rows_of(g), 0:CH], win[0], NT)
         for j in (1, 2):
             partial += mm(gg[rows_of(g), j * CH : (j + 1) * CH], win[j], NT)
-        for k in range(2):
-            part[0, 2 * g + k] = partial[k * TB : (k + 1) * TB]
-            sum_begin(2, 2 * g + k)
-
-    outs = []
+        part[0, 2 * g : 2 * g + 2] = partial.reshape(2, TB, D)
+        sum_begin(2, g)
 
     def tokens_out(r):
         t, grad = tok[r], part[0, r]
@@ -522,35 +574,33 @@
             + scale * weighted
             - t * (scale * scale * scale) * jnp.mean(weighted * t, axis=-1, keepdims=True)
         )
-        outs.append(pltpu.make_async_copy(cot.at[r], grad_tokens.at[r], out_sem.at[r]))
-        outs[-1].start()
+        leave(cot.at[r], grad_tokens.at[r])
 
     def result_out(r):
         mid[r] = mid[r] + part[1, r]
-        outs.append(pltpu.make_async_copy(mid.at[r], result.at[r], out_sem.at[4 + r]))
-        outs[-1].start()
+        leave(mid.at[r], result.at[r])
 
     reduced = {}
 
     def small_begin(stage):
         at, peers = (
+            (l, [across]),
             (y, [dev(y=up(y, k)) for k in (1, 2, 3)]),
             (z, [dev(z=up(z, k)) for k in (1, 2, 3)]),
-            (l, [across]),
         )[stage]
         ar[stage, at] = small[...]
         reduced[stage] = [
-            remote(small, ar.at[stage, at], ar_s.at[stage, k], ar_r.at[stage, at], to)
+            remote(small, ar.at[stage, at], ar_s.at[k], ar_r.at[stage, at], to)
             for k, to in enumerate(peers)
         ]
 
     def small_end(stage):
-        at, count = ((y, 4), (z, 4), (l, 2))[stage]
+        at, count = ((l, 2), (y, 4), (z, 4))[stage]
         for k, copy in enumerate(reduced[stage]):
             copy.wait_send()
             there = (at + k + 1) % count
             pltpu.make_async_remote_copy(
-                src_ref=small, dst_ref=ar.at[stage, there], send_sem=ar_s.at[stage, k],
+                src_ref=small, dst_ref=ar.at[stage, there], send_sem=ar_s.at[k],
                 recv_sem=ar_r.at[stage, there], device_id=mate, device_id_type=MESH,
             ).wait_recv()
         total = ar[stage, 0] + ar[stage, 1]
@@ -560,15 +610,14 @@
 
     loads["wout"].wait()
     weight_begin()
-    pl.semaphore_wait(barrier, len(partners))
-    weight_far()
     loads["tok"].wait()
     loads["win"].wait()
     mixer_in(0)
-    send_halo(0)
+    pl.semaphore_wait(barrier, len(partners))
+    weight_far()
     mixer_out(0)
     mixer_in(1)
-    send_halo(1)
+    send_halo()
     mixer_out(1)
     weight_first()
     loads["cot"].wait()
@@ -578,138 +627,145 @@
     weight_second()
     mixer_edge()
     mix_pass(0)
+    weight_near()
+    for k in range(3):
+        mix_near(k)
+    branch(h, tok)
     mix_pass(1)
+    weight_third()
     mix_pass(2)
-    weight_third()
-    mix_pass(3)
-    mix_pass(4)
     loads["wg"].wait()
     loads["wu"].wait()
+    for k in range(3):
+        mix_end(k)
     weight_end()
-    mix_end(0)
-    mix_end(1)
-    mix_end(4)
-    branch(0)
-    ffn(0)
-    mix_end(2)
-    mix_end(3)
-    branch(1)
-    ffn(1)
-    product(0, gf, hid[...], 0, HID)
-    ring_begin(0)
+    branch(1 - h, mid)
+    ffn_norm()
+    for tile in TILES[:2]:
+        ffn_tiles([tile])
+        product_down([tile])
+    ring_begin(0, (0, 512))
+    ffn_tiles(TILES[2:])
+    product_down(TILES[2:])
+    ring_begin(0, (512, 640))
+    ring_fill(0)
     ffn_back(0)
     ffn_back(1)
-    for r in range(4):
-        sum_cross(1, r)
+    sum_cross(1, 0)
+    sum_cross(1, 1)
     product(1, aff, gg[...], 0, HID)
     ring_relay(0)
     ring_begin(1)
+    ring_fill(1)
     sum_share(1, 0)
-    sum_share(1, 1)
     sum_end(1, 0)
-    sum_end(1, 1)
     mixer_back(0)
     ring_turn(0)
     ring_sent(0, first)
     product(0, aff, gu[...], 0, HID)
     ffn_out(0)
-    sum_share(1, 2)
     sum_cross(3, 0)
-    sum_cross(3, 1)
     ring_relay(1)
     ring_begin(2)
-    sum_share(1, 3)
-    sum_end(1, 2)
-    sum_end(1, 3)
+    sum_share(1, 1)
+    sum_end(1, 1)
     mixer_back(1)
-    product(None, gf, wg[0:POS, 0:CH], 0, CH)
+    product_out()
     pair_begin()
     mixer_back_in(0)
+    ring_fill(2)
     ffn_out(1)
     sum_cross(2, 0)
-    sum_cross(2, 1)
     ring_relay_two(0)
     mixer_back_in(1)
     ring_turn(1)
     ring_sent(1, first)
-    sum_cross(2, 2)
-    sum_cross(2, 3)
+    sum_cross(2, 1)
     for g in (0, 1):
         aff[rows_of(g)] = normed(g)
     product(1, aff, gg[:, 0 : 3 * CH], 0, 3 * CH)
+    ring_begin(3)
     ring_relay(2)
-    ring_begin(3)
     pair_end()
     ring_begin(4)
     ring_cross(0)
+    sum_share(3, 0)
+    sum_end(3, 0)
+    result_out(0)
+    result_out(1)
     ring_relay_two(1)
-    sum_share(3, 0)
-    sum_share(3, 1)
-    sum_cross(3, 2)
-    sum_cross(3, 3)
+    ring_fill(3)
+    ring_fill(4)
     sum_share(2, 0)
+    sum_cross(3, 1)
     ring_sent(0, second)
     ring_relay(3)
+    sum_end(2, 0)
+    for r in (0, 1):
+        tokens_out(r)
+    ring_turn(2)
     ring_relay(4)
     sum_share(2, 1)
-    for r in (0, 1):
-        sum_end(3, r)
-        result_out(r)
-        sum_end(2, r)
+    sum_end(2, 1)
+    for r in (2, 3):
         tokens_out(r)
+    small_begin(0)
     ring_cross(1)
     ring_sent(1, second)
-    ring_turn(2)
-    sum_share(2, 2)
+    ring_turn(3)
     ring_relay_two(2)
-    ring_turn(3)
     ring_turn(4)
-    sum_share(2, 3)
-    for r in (2, 3):
-        sum_end(2, r)
-        tokens_out(r)
-    small_begin(0)
-    ring_cross(2)
-    ring_relay_two(3)
-    ring_relay_two(4)
     small_end(0)
     small_begin(1)
+    ring_cross(3)
+    small_end(1)
+    small_begin(2)
+    ring_cross(2)
+    ring_cross(4)
+    sum_share(3, 1)
+    sum_end(3, 1)
+    for r in (2, 3):
+        result_out(r)
     ring_end(0)
     ring_end(1)
-    ring_cross(3)
-    ring_cross(4)
-    small_end(1)
-    small_begin(2)
-    sum_share(3, 2)
-    sum_share(3, 3)
-    for r in (2, 3):
-        sum_end(3, r)
-        result_out(r)
+    small_end(2)
+    leave(small, o_small)
+    for job in range(2, 5):
+        ring_sent(job, first)
+        ring_sent(job, second)
+    ring_end(3)
     ring_end(2)
-    small_end(2)
-    o_small[...] = small[...]
-    for job in range(5):
-        if job >= 2:
-            ring_sent(job, first)
-            ring_sent(job, second)
-    ring_end(3)
     for copy in outs:
         copy.wait()
 
 
 def finish(*refs):
-    ins, outs = refs[:8], refs[8:]
-    outs[0][...] = ins[0][...]
-    outs[1][...] = ins[1][...]
-
-    @pl.when(pl.program_id(0) == 0)
-    def _():
-        for src, dst in zip(ins[2:7], outs[2:7]):
-            dst[...] = src[...]
-        small = ins[7]
-        outs[7][...] = small[1]
-        outs[8][...] = small[0]
-        outs[9][...] = small[2:5, 0:CH]
+    ins, outs, held, sem = refs[:8], refs[8:18], refs[18:28], refs[28]
+    parts = [(k, r) for r in range(ROWS) for k in range(2)] + [(k, None) for k in range(2, 10)]
+
+    def move(way, n):
+        k, r = parts[n]
+        src, dst = ((ins, held), (held, outs))[way]
+        if r is None:
+            return pltpu.make_async_copy(src[k], dst[k], sem.at[way, n])
+        return pltpu.make_async_copy(src[k].at[r], dst[k].at[r], sem.at[way, n])
+
+    incoming = [move(0, n) for n in range(13)]
+    for copy in incoming:
+        copy.start()
+    small = ins[7]
+    held[7][...] = small[1]
+    held[8][...] = small[0]
+    held[9][...] = small[2:5, 0:CH]
+    outgoing = [move(1, n) for n in range(13, 16)]
+    for copy in outgoing:
+        copy.start()
+    for n, copy in enumerate(incoming):
+        copy.wait()
+        outgoing.append(move(1, n))
+        outgoing[-1].start()
+    for copy in outgoing:
+        copy.wait()
 
 
 def on_device(
@@ -732,7 +788,7 @@
             shape((8, D), F32),
         ),
         in_specs=[pl.BlockSpec(memory_space=pltpu.SMEM)] + [any_spec] * 7 + [vmem] * 3,
-        out_specs=(any_spec, any_spec) + (vmem,) * 6,
+        out_specs=(any_spec,) * 8,
         scratch_shapes=[
             pltpu.VMEM((ROWS, TB, D), F32),
             pltpu.VMEM((ROWS, TB, D), F32),
@@ -749,7 +805,7 @@
             pltpu.VMEM((POS, HID), BF16),
             pltpu.VMEM((POS, HID), BF16),
             pltpu.VMEM((POS, HID), BF16),
-            pltpu.VMEM((POS, D), BF16),
+            pltpu.VMEM((2, POS, POS), BF16),
             pltpu.VMEM((POS, HID), F32),
                 pltpu.VMEM((ROWS, 8, CH), F32),
             pltpu.VMEM((ROWS, 8, CH), F32),
@@ -769,28 +825,30 @@
             pltpu.VMEM((8, D), F32),
             pltpu.VMEM((3, 4, 8, D), F32),
             dma((7,)),
-            dma((8,)),
-            dma((3, 5)),
-            dma((3, 5)),
+            dma((16,)),
+            dma((3, 3)),
+            dma((3, 3)),
             dma((22,)),
             dma((22,)),
+            dma((3,)),
+            dma((3,)),
+            dma((2, 2)),
+            dma((3, 2)),
+            dma((2, 2)),
+            dma((3, 2)),
+            dma((2, 2)),
+            dma((3, 2)),
+            dma((3, 2, 6)),
+            dma((3, 2, 6)),
             dma((2, 4)),
             dma((2, 4)),
-            dma((4, 4)),
-            dma((4, 4)),
-            dma((4, 4)),
-            dma((4, 4)),
-            dma((4, 4)),
-            dma((4, 4)),
-            dma((5, 2, 6)),
-            dma((5, 2, 6)),
-            dma((5, 2, 6)),
+            dma((3, 2, 6)),
             dma((5, 2, 6)),
             dma((4,)),
             dma((4,)),
             dma((1,)),
             dma((1,)),
-            dma((3, 3)),
+            dma((3,)),
             dma((3, 4)),
             pltpu.SemaphoreType.REGULAR((2, 2, 2)),
         ],
@@ -802,11 +860,6 @@
         start_flags.T, tokens, cotangent, w_in, w_out, w_gate, w_up, w_down,
         norm_one.reshape(1, D), norm_two.reshape(1, D), w_conv,
     )
-    row = pl.BlockSpec((1, TB, D), lambda r: (r, 0, 0))
-
-    def whole(array):
-        return pl.BlockSpec(array.shape, lambda r: (0,) * array.ndim)
-
     result, grad_tokens, g_in, g_out, g_gate, g_up, g_down, one, two, taps = pl.pallas_call(
         finish,
         out_shape=tuple(shape(o.shape, F32) for o in outs[:2])
@@ -820,10 +873,12 @@
             shape((D,), F32),
             shape((3, CH), F32),
         ),
-        grid=(ROWS,),
-        in_specs=[row, row] + [whole(o) for o in outs[2:]],
-        out_specs=(row, row) + tuple(whole(o) for o in outs[2:7])
-        + (pl.BlockSpec((D,), lambda r: (0,)),) * 2 + (pl.BlockSpec((3, CH), lambda r: (0, 0)),),
+        in_specs=[any_spec] * 7 + [vmem],
+        out_specs=(any_spec,) * 10,
+        scratch_shapes=[pltpu.VMEM(o.shape, F32) for o in outs[:7]]
+        + [pltpu.VMEM(d, F32) for d in ((D,), (D,), (3, CH))]
+        + [dma((2, 16))],
+        compiler_params=pltpu.CompilerParams(vmem_limit_bytes=60 * 2**20),
         name="finish",
     )(*outs)
     return result, grad_tokens, one, g_in, taps, g_out, two, g_gate, g_up, g_down

time: 147 us -> 139 us (0.946); the launches traced: 145 us -> 139 us
  Pallas kernels: 144 us -> 138 us
    pallas_call x1, Pallas kernels: 139 us -> 133 us  [on_device(): pl.pallas_call(kernel, out_shape=(shape((ROWS, TB, D), F32), shape((ROWS,...]
where the time goes in v3:
time: 139 us
  Pallas kernels  138 us (99%)
    pallas_call x1, Pallas kernels, on_device(): pl.pallas_call(kernel, out_shape=(shape((ROWS, TB, D), F32), shape((ROWS,...  133 us
    pallas_call x1, Pallas kernels, on_device(): pl.pallas_call(finish, out_shape=tuple((shape(o.shape, F32) for o in outs...  4.94 us

profile of v3, /device:TPU:0, one launch (start us, length us, event | category | flops | bytes accessed | tf_op | source)
XLA Modules:
  0.0 139.0 jit_solution(14425829386061695161)
XLA Ops:
  0.6 133.2 %block.1 = (f32[4,128,1024]{2,1,0:T(8,128)}, f32[4,128,1024]{2,1,0:T(8,128)}, f32[3,32,256]{2,1,0:T(8,128)}, f32[32,256]{1,0:T(8,128)}, f32[32,1152]{1,0:T(8,128...) custom-call(s32[1,4]{1,0:T(1,128)} %bitcast.5, f32[4,128,1024]{2,1,0:T(8,128)} %tokens.1, ...), custom_call_target="tpu_custom_call" | custom-call | tf_op jit(solution)/shard_map/block/pallas_call | solution.py:778
  133.9 4.9 %finish.1 = (f32[4,128,1024]{2,1,0:T(8,128)}, f32[4,128,1024]{2,1,0:T(8,128)}, f32[3,32,256]{2,1,0:T(8,128)}, f32[32,256]{1,0:T(8,128)}, f32[32,1152]{1,0:T(8,12...) custom-call(f32[4,128,1024]{2,1,0:T(8,128)} %get-tuple-element.28.refs_0_, ...), custom_call_target="tpu_custom_call" | custom-call | tf_op jit(solution)/shard_map/finish/pallas_call | solution.py:863

commit v4 on v3

--- a/solution.py
+++ b/solution.py
@@ -717,17 +717,17 @@
     ring_turn(4)
     small_end(0)
     small_begin(1)
+    sum_share(3, 1)
     ring_cross(3)
+    ring_end(0)
+    ring_end(1)
     small_end(1)
     small_begin(2)
     ring_cross(2)
     ring_cross(4)
-    sum_share(3, 1)
     sum_end(3, 1)
     for r in (2, 3):
         result_out(r)
-    ring_end(0)
-    ring_end(1)
     small_end(2)
     leave(small, o_small)
     for job in range(2, 5):

time: 139 us -> 139 us (level)
  no operation moved by 1% of the time
where the time goes in v4:
time: 139 us
  Pallas kernels  138 us (99%)
    pallas_call x1, Pallas kernels, on_device(): pl.pallas_call(kernel, out_shape=(shape((ROWS, TB, D), F32), shape((ROWS,...  133 us
    pallas_call x1, Pallas kernels, on_device(): pl.pallas_call(finish, out_shape=tuple((shape(o.shape, F32) for o in outs...  4.94 us

profile of v4, /device:TPU:0, one launch (start us, length us, event | category | flops | bytes accessed | tf_op | source)
XLA Modules:
  0.0 139.0 jit_solution(3657297499892212626)
XLA Ops:
  0.6 133.3 %block.1 = (f32[4,128,1024]{2,1,0:T(8,128)}, f32[4,128,1024]{2,1,0:T(8,128)}, f32[3,32,256]{2,1,0:T(8,128)}, f32[32,256]{1,0:T(8,128)}, f32[32,1152]{1,0:T(8,128...) custom-call(s32[1,4]{1,0:T(1,128)} %bitcast.5, f32[4,128,1024]{2,1,0:T(8,128)} %tokens.1, ...), custom_call_target="tpu_custom_call" | custom-call | tf_op jit(solution)/shard_map/block/pallas_call | solution.py:778
  133.9 4.9 %finish.1 = (f32[4,128,1024]{2,1,0:T(8,128)}, f32[4,128,1024]{2,1,0:T(8,128)}, f32[3,32,256]{2,1,0:T(8,128)}, f32[32,256]{1,0:T(8,128)}, f32[32,1152]{1,0:T(8,12...) custom-call(f32[4,128,1024]{2,1,0:T(8,128)} %get-tuple-element.28.refs_0_, ...), custom_call_target="tpu_custom_call" | custom-call | tf_op jit(solution)/shard_map/finish/pallas_call | solution.py:863

commit v5 on v4

--- a/solution.py
+++ b/solution.py
@@ -697,7 +697,6 @@
     ring_fill(3)
     ring_fill(4)
     sum_share(2, 0)
-    sum_cross(3, 1)
     ring_sent(0, second)
     ring_relay(3)
     sum_end(2, 0)
@@ -710,19 +709,20 @@
     for r in (2, 3):
         tokens_out(r)
     small_begin(0)
+    sum_cross(3, 1)
     ring_cross(1)
     ring_sent(1, second)
     ring_turn(3)
+    small_end(0)
+    small_begin(1)
     ring_relay_two(2)
     ring_turn(4)
-    small_end(0)
-    small_begin(1)
-    sum_share(3, 1)
     ring_cross(3)
+    small_end(1)
+    small_begin(2)
     ring_end(0)
     ring_end(1)
-    small_end(1)
-    small_begin(2)
+    sum_share(3, 1)
     ring_cross(2)
     ring_cross(4)
     sum_end(3, 1)

time: 139 us -> 141 us (1.014)
  Pallas kernels: 138 us -> 140 us
    pallas_call x1, Pallas kernels: 133 us -> 135 us  [on_device(): pl.pallas_call(kernel, out_shape=(shape((ROWS, TB, D), F32), shape((ROWS,...]
where the time goes in v5:
time: 141 us
  Pallas kernels  140 us (99%)
    pallas_call x1, Pallas kernels, on_device(): pl.pallas_call(kernel, out_shape=(shape((ROWS, TB, D), F32), shape((ROWS,...  135 us
    pallas_call x1, Pallas kernels, on_device(): pl.pallas_call(finish, out_shape=tuple((shape(o.shape, F32) for o in outs...  4.94 us

profile of v5, /device:TPU:0, one launch (start us, length us, event | category | flops | bytes accessed | tf_op | source)
XLA Modules:
  0.0 141.1 jit_solution(9774165789044172281)
XLA Ops:
  0.6 135.3 %block.1 = (f32[4,128,1024]{2,1,0:T(8,128)}, f32[4,128,1024]{2,1,0:T(8,128)}, f32[3,32,256]{2,1,0:T(8,128)}, f32[32,256]{1,0:T(8,128)}, f32[32,1152]{1,0:T(8,128...) custom-call(s32[1,4]{1,0:T(1,128)} %bitcast.5, f32[4,128,1024]{2,1,0:T(8,128)} %tokens.1, ...), custom_call_target="tpu_custom_call" | custom-call | tf_op jit(solution)/shard_map/block/pallas_call | solution.py:778
  136.0 4.9 %finish.1 = (f32[4,128,1024]{2,1,0:T(8,128)}, f32[4,128,1024]{2,1,0:T(8,128)}, f32[3,32,256]{2,1,0:T(8,128)}, f32[32,256]{1,0:T(8,128)}, f32[32,1152]{1,0:T(8,12...) custom-call(f32[4,128,1024]{2,1,0:T(8,128)} %get-tuple-element.28.refs_0_, ...), custom_call_target="tpu_custom_call" | custom-call | tf_op jit(solution)/shard_map/finish/pallas_call | solution.py:863
